TPU v7x, 128 devices: a whole 4x4x4 slice. The times are simulated.
128 devices in a mesh: dp: 16 (over z, x_hi, core), seq: 8 (over y, x_lo).
Axes of the slice: x: 4 (x_hi: 2, x_lo: 2; x = x_hi * 2 + x_lo), y: 4, z: 4, core: 2. Of those that a mesh axis runs over, the one named last changes fastest.
Arguments:
- inputs: bfloat16 [32, 1024, 576], P('dp', 'seq'), may hold values from -6 to 6
- segment_ids: int32 [32, 1024], P('dp'), may hold values from 0 to 64, as said below
- norm_attn: bfloat16 [576], P('dp'), may hold values from 0.5 to 1.5
- w_query: bfloat16 [576, 576], P('dp'), may hold values from -0.25 to 0.25
- w_key: bfloat16 [576, 192], P('dp'), may hold values from -0.25 to 0.25
- w_value: bfloat16 [576, 192], P('dp'), may hold values from -0.25 to 0.25
- w_out: bfloat16 [576, 576], P('dp'), may hold values from -1 to 1
- norm_mlp: bfloat16 [576], P('dp'), may hold values from 0.5 to 1.5
- w_gate: bfloat16 [576, 1536], P(None, ('dp', 'seq')), may hold values from -0.25 to 0.25
- w_up: bfloat16 [576, 1536], P(None, ('dp', 'seq')), may hold values from -0.25 to 0.25
- w_down: bfloat16 [1536, 576], P(('dp', 'seq')), may hold values from -0.15625 to 0.15625
- cotangent: bfloat16 [32, 1024, 576], P('dp', 'seq'), may hold values from -6 to 6
Outputs:
- output: bfloat16 [32, 1024, 576], P('dp', 'seq')
- grad_inputs: bfloat16 [32, 1024, 576], P('dp', 'seq')
- grad_norm_attn: float32 [576], P('dp')
- grad_w_query: float32 [576, 576], P('dp')
- grad_w_key: float32 [576, 192], P('dp')
- grad_w_value: float32 [576, 192], P('dp')
- grad_w_out: float32 [576, 576], P('dp')
- grad_norm_mlp: float32 [576], P('dp')
- grad_w_gate: float32 [576, 1536], P(None, ('dp', 'seq'))
- grad_w_up: float32 [576, 1536], P(None, ('dp', 'seq'))
- grad_w_down: float32 [1536, 576], P(('dp', 'seq'))
Inputs may be any that keep to these rules, and one draw needn't show every extreme that they name: `segment_ids`: each row starts at 0, never falls and rises by at most one from one position to the next, and its last id is exactly 64; in every sequence one document covers positions 127 through 1024 - 128.
All inputs are finite; a program needn't handle non-finite values.
Results may differ from a plain program's by a relative error of at most 0.023.
Values may be sent and summed in bfloat16 or wider, within the bound.
A program may use at most 128 MiB of HBM per device.

v0:
```python
import jax
import jax.numpy as jnp
from jax import lax
from jax.sharding import PartitionSpec as P

QUERY_HEADS = 9
KV_HEADS = 3
HEAD_WIDTH = 64


ROPE_BASE = 100000.0
NORM_EPS = 1e-05
MASKED = -1e30


def in_one_piece(arrays, axis, dim, along):
    columns = [a.reshape(*a.shape[:along], -1) for a in arrays]
    both = jnp.concatenate(columns, axis=along)
    whole, at, outs = (lax.all_gather(both, axis, axis=dim, tiled=True), 0, [])
    for a, column in zip(arrays, columns):
        section = whole[..., at : at + column.shape[along]]
        outs.append(section.reshape(*section.shape[:along], *a.shape[along:]))
        at += column.shape[along]
    return tuple(outs)


def gather_turned(arrays, axis, dims):
    turned = [jnp.moveaxis(a, dim, 0) for a, dim in zip(arrays, dims)]
    widths = [t[0].size for t in turned]
    both = jnp.concatenate([t.reshape(-1, w) for t, w in zip(turned, widths)], axis=1)
    whole = lax.all_gather(both, axis, axis=0, tiled=True)
    parts = jnp.split(whole, [sum(widths[:k]) for k in range(1, len(widths))], axis=1)
    return tuple(
        (
            jnp.moveaxis(b.reshape(-1, *t.shape[1:]), 0, dim)
            for b, t, dim in zip(parts, turned, dims)
        )
    )


def joined_along(parts, dim):
    parts = jnp.moveaxis(parts, 0, dim)
    lengths = parts.shape
    return parts.reshape(*lengths[:dim], lengths[dim] * lengths[dim + 1], *lengths[dim + 2 :])


def copy_for_each(x, axis):
    length = lax.axis_size(axis)
    return lax.all_to_all(jnp.broadcast_to(x[None], (length, *x.shape)), axis, 0, 0, tiled=True)


def collect(x, axis, dim):
    return joined_along(copy_for_each(x, axis), dim)


def in_blocks(x, dim, length):
    lengths = x.shape
    parts = x.reshape(*lengths[:dim], length, lengths[dim] // length, *lengths[dim + 1 :])
    return jnp.moveaxis(parts, dim, 0)


def summed_on_arrival(x, axis, dim):
    parts = in_blocks(x, dim, lax.axis_size(axis))
    arrived = lax.all_to_all(parts, axis, split_axis=0, concat_axis=0, tiled=True)
    return arrived.astype(jnp.float32).sum(axis=0)


def sum_packed(arrays, axis, dims):
    length = lax.axis_size(axis)
    parts = [in_blocks(a, dim, length) for a, dim in zip(arrays, dims)]
    lines = jnp.concatenate([b.reshape(length, -1) for b in parts], axis=1)
    rows = max(16, -(-lines.shape[1] // 1024) * 8)
    lines = jnp.pad(lines, ((0, 0), (0, rows * 128 - lines.shape[1]))).reshape(-1, 128)
    vector, at, outs = (lax.psum_scatter(lines, axis, tiled=True).reshape(-1), 0, [])
    for b in parts:
        part = b[0]
        outs.append(vector[at : at + part.size].reshape(part.shape))
        at += part.size
    return tuple(outs)


def taken_together(x, axis):
    return copy_for_each(x, axis).astype(jnp.float32).sum(axis=0)


def dot_plain(left_side, right_side):
    return jnp.dot(left_side, right_side, preferred_element_type=jnp.float32)


def dot_first(left_side, right_side):
    return lax.dot_general(
        left_side, right_side, (((0,), (0,)), ((), ())), preferred_element_type=jnp.float32
    )


def dot_second(left_side, right_side):
    return lax.dot_general(
        left_side, right_side, (((1,), (1,)), ((), ())), preferred_element_type=jnp.float32
    )


def norm_forward(value_rows, gain_row):
    inv_root = lax.rsqrt(jnp.mean(value_rows * value_rows, axis=-1, keepdims=True) + NORM_EPS)
    unit_rows = value_rows * inv_root
    return (unit_rows, inv_root, unit_rows * gain_row)


def norm_backward(grad_rows, unit_rows, inv_root, gain_row):
    scaled = grad_rows * gain_row
    row_inner = jnp.mean(scaled * unit_rows, axis=-1, keepdims=True)
    return (inv_root * (scaled - unit_rows * row_inner), jnp.sum(grad_rows * unit_rows, axis=0))


def rotary(positions):
    half_dim = HEAD_WIDTH // 2
    frequency = ROPE_BASE ** (-(2.0 * jnp.arange(half_dim, dtype=jnp.float32)) / HEAD_WIDTH)
    angles = positions.astype(jnp.float32)[:, None] * frequency[None, :]
    return (jnp.cos(angles)[:, None, :], jnp.sin(angles)[:, None, :])


def rotate(vectors, cosine_table, sine_table):
    half_dim = vectors.shape[-1] // 2
    first_half = vectors[..., :half_dim]
    second = vectors[..., half_dim:]
    return jnp.concatenate(
        [
            first_half * cosine_table - second * sine_table,
            second * cosine_table + first_half * sine_table,
        ],
        axis=-1,
    )


def masked_scores(query_rows, key_rows_gathered, allowed):
    score_matrix = jnp.einsum(
        "aymo,zyo->ymaz", query_rows, key_rows_gathered, preferred_element_type=jnp.float32
    ) * HEAD_WIDTH ** (-0.5)
    return jnp.where(allowed[None, None], score_matrix, MASKED)


def local(
    inputs,
    segment_ids,
    norm_attn,
    w_query,
    w_key,
    w_value,
    w_out,
    norm_mlp,
    w_gate,
    w_up,
    w_down,
    cotangent,
):
    attn_shards = (norm_attn, w_query, w_key, w_value, w_out, norm_mlp)
    data_count = lax.axis_size("dp")
    devices = lax.axis_size("dp") * lax.axis_size("seq")
    seq_rank = lax.axis_index("seq")
    local_len = inputs.shape[1]
    full_len = segment_ids.shape[1]
    group_size = QUERY_HEADS // KV_HEADS
    kv_width = KV_HEADS * HEAD_WIDTH
    local_index = seq_rank * local_len + jnp.arange(local_len, dtype=jnp.int32)
    key_index = jnp.arange(full_len, dtype=jnp.int32)
    start_sums = (
        tuple(
            (
                jnp.zeros(
                    (weight_shard.shape[0] * data_count,) + weight_shard.shape[1:], jnp.float32
                )
                for weight_shard in attn_shards
            )
        ),
        (
            jnp.zeros((w_gate.shape[0], w_gate.shape[1] * devices), jnp.float32),
            jnp.zeros((w_up.shape[0], w_up.shape[1] * devices), jnp.float32),
            jnp.zeros((w_down.shape[0] * devices, w_down.shape[1]), jnp.float32),
        ),
    )

    def micro(grad_sums, batch_item):
        tokens, segments, grad_out = batch_item
        attn_full = in_one_piece((norm_attn, w_query, w_key, w_value, w_out, norm_mlp), "dp", 0, 1)
        mlp_full = gather_turned((w_gate, w_up, w_down), ("dp", "seq"), (1, 1, 0))
        gain_attn, query_w, key_w, value_w, out_w, gain_mlp = attn_full
        gate_w, up_w, down_w = mlp_full
        hidden = tokens.astype(jnp.float32)
        own_segs = lax.dynamic_slice_in_dim(segments, seq_rank * local_len, local_len)
        earlier = jnp.sum((segments[None, :] < own_segs[:, None]).astype(jnp.int32), axis=1)
        cosine_table, sine_table = rotary(local_index - earlier)
        allowed = (own_segs[:, None] == segments[None, :]) & (
            key_index[None, :] <= local_index[:, None]
        )
        unit_one, root_one, normed_one = norm_forward(hidden, gain_attn.astype(jnp.float32))
        normed_low = normed_one.astype(jnp.bfloat16)
        query_pre = dot_plain(normed_low, query_w)
        key_pre = dot_plain(normed_low, key_w)
        value_pre = dot_plain(normed_low, value_w)
        query_rows = rotate(
            query_pre.reshape(local_len, QUERY_HEADS, HEAD_WIDTH), cosine_table, sine_table
        ).astype(jnp.bfloat16)
        query_rows = query_rows.reshape(local_len, KV_HEADS, group_size, HEAD_WIDTH)
        keys_own = rotate(
            key_pre.reshape(local_len, KV_HEADS, HEAD_WIDTH), cosine_table, sine_table
        ).astype(jnp.bfloat16)
        keys_own = keys_own.reshape(local_len, kv_width)
        values_own = value_pre.astype(jnp.bfloat16)
        stacked_own = jnp.concatenate([keys_own, values_own], axis=1)
        stacked_all = collect(stacked_own, "seq", 0)
        key_rows_gathered = stacked_all[:, :kv_width].reshape(full_len, KV_HEADS, HEAD_WIDTH)
        value_rows_gathered = stacked_all[:, kv_width:].reshape(full_len, KV_HEADS, HEAD_WIDTH)
        score_matrix = masked_scores(query_rows, key_rows_gathered, allowed)
        row_top = jnp.max(score_matrix, axis=-1, keepdims=True)
        log_total = row_top + jnp.log(
            jnp.sum(jnp.exp(score_matrix - row_top), axis=-1, keepdims=True)
        )
        attention_output = jnp.exp(score_matrix - log_total).astype(jnp.bfloat16)
        merged_heads = jnp.einsum(
            "moei,imz->emoz",
            attention_output,
            value_rows_gathered,
            preferred_element_type=jnp.float32,
        )
        merged_heads = merged_heads.reshape(local_len, QUERY_HEADS * HEAD_WIDTH).astype(
            jnp.bfloat16
        )
        middle = hidden + dot_plain(merged_heads, out_w)
        unit_two, root_two, normed_two = norm_forward(middle, gain_mlp.astype(jnp.float32))
        normed_mid = normed_two.astype(jnp.bfloat16)
        gate_value = dot_plain(normed_mid, gate_w)
        up_value = dot_plain(normed_mid, up_w)
        sigmoid_gate = jax.nn.sigmoid(gate_value)
        silu_gate = gate_value * sigmoid_gate
        activated = (silu_gate * up_value).astype(jnp.bfloat16)
        result = middle + dot_plain(activated, down_w)
        grad_down_w = dot_first(activated, grad_out)
        grad_act = dot_second(grad_out, mlp_full[2])
        grad_gate = (
            grad_act * up_value * sigmoid_gate * (1.0 + gate_value * (1.0 - sigmoid_gate))
        ).astype(jnp.bfloat16)
        grad_up = (grad_act * silu_gate).astype(jnp.bfloat16)
        grad_gate_w = dot_first(normed_mid, grad_gate)
        grad_up_w = dot_first(normed_mid, grad_up)
        grad_normed_two = dot_second(grad_gate, mlp_full[0]) + dot_second(grad_up, mlp_full[1])
        grad_mid_norm, grad_gain_mlp = norm_backward(
            grad_normed_two, unit_two, root_two, attn_full[5].astype(jnp.float32)
        )
        grad_middle = grad_out.astype(jnp.float32) + grad_mid_norm
        grad_branch = grad_middle.astype(jnp.bfloat16)
        grad_out_w = dot_first(merged_heads, grad_branch)
        gradient_merged_heads = dot_second(grad_branch, attn_full[4]).astype(jnp.bfloat16)
        gradient_merged_heads = gradient_merged_heads.reshape(
            local_len, KV_HEADS, group_size, HEAD_WIDTH
        )
        scores_again = masked_scores(query_rows, key_rows_gathered, allowed)
        attention_again = jnp.exp(scores_again - log_total)
        grad_values = jnp.einsum(
            "fiyn,yfic->nfc",
            attention_again.astype(jnp.bfloat16),
            gradient_merged_heads,
            preferred_element_type=jnp.float32,
        )
        grad_attention = jnp.einsum(
            "aymo,zyo->ymaz",
            gradient_merged_heads,
            value_rows_gathered,
            preferred_element_type=jnp.float32,
        )
        row_inner = jnp.sum(attention_again * grad_attention, axis=-1, keepdims=True)
        gradient_score_matrix = (attention_again * (grad_attention - row_inner)).astype(
            jnp.bfloat16
        )
        grad_queries = jnp.einsum(
            "moei,imz->emoz",
            gradient_score_matrix,
            key_rows_gathered,
            preferred_element_type=jnp.float32,
        ) * HEAD_WIDTH ** (-0.5)
        grad_keys = jnp.einsum(
            "fiyn,yfic->nfc", gradient_score_matrix, query_rows, preferred_element_type=jnp.float32
        ) * HEAD_WIDTH ** (-0.5)
        stacked_grads = jnp.concatenate(
            [grad_keys.reshape(full_len, kv_width), grad_values.reshape(full_len, kv_width)], axis=1
        )
        stacked_own_grads = summed_on_arrival(stacked_grads.astype(jnp.bfloat16), "seq", 0)
        grad_keys_own = stacked_own_grads[:, :kv_width]
        grad_values_own = stacked_own_grads[:, kv_width:]
        grad_query_pre = rotate(
            grad_queries.reshape(local_len, QUERY_HEADS, HEAD_WIDTH), cosine_table, -sine_table
        )
        grad_query_pre = grad_query_pre.reshape(local_len, QUERY_HEADS * HEAD_WIDTH).astype(
            jnp.bfloat16
        )
        grad_key_pre = rotate(
            grad_keys_own.reshape(local_len, KV_HEADS, HEAD_WIDTH), cosine_table, -sine_table
        )
        grad_key_pre = grad_key_pre.reshape(local_len, kv_width).astype(jnp.bfloat16)
        grad_value_pre = grad_values_own.astype(jnp.bfloat16)
        grad_normed_one = (
            dot_second(grad_query_pre, attn_full[1])
            + dot_second(grad_key_pre, attn_full[2])
            + dot_second(grad_value_pre, attn_full[3])
        )
        grad_in_norm, grad_gain_attn = norm_backward(
            grad_normed_one, unit_one, root_one, attn_full[0].astype(jnp.float32)
        )
        grad_tokens = (grad_middle + grad_in_norm).astype(jnp.bfloat16)
        attn_terms = (
            grad_gain_attn,
            dot_first(normed_low, grad_query_pre),
            dot_first(normed_low, grad_key_pre),
            dot_first(normed_low, grad_value_pre),
            grad_out_w,
            grad_gain_mlp,
        )
        mlp_terms = (grad_gate_w, grad_up_w, grad_down_w)
        new_sums = jax.tree.map(jnp.add, grad_sums, (attn_terms, mlp_terms))
        return (new_sums, (result.astype(jnp.bfloat16), grad_tokens))

    grad_sums, (outputs, grad_inputs) = lax.scan(
        micro, start_sums, (inputs, segment_ids, cotangent)
    )
    attn_sum, mlp_sum = grad_sums
    attn_rows = tuple(
        (
            part.astype(jnp.float32)
            for part in sum_packed(
                (
                    attn_sum[0].astype(jnp.bfloat16),
                    attn_sum[1].astype(jnp.bfloat16),
                    attn_sum[2].astype(jnp.bfloat16),
                    attn_sum[3].astype(jnp.bfloat16),
                    attn_sum[4].astype(jnp.bfloat16),
                    attn_sum[5].astype(jnp.bfloat16),
                ),
                "dp",
                (0, 0, 0, 0, 0, 0),
            )
        )
    )
    attn_done = (
        taken_together(attn_rows[0].astype(jnp.bfloat16), "seq").astype(jnp.float32),
        taken_together(attn_rows[1].astype(jnp.bfloat16), "seq").astype(jnp.float32),
        taken_together(attn_rows[2].astype(jnp.bfloat16), "seq").astype(jnp.float32),
        taken_together(attn_rows[3].astype(jnp.bfloat16), "seq").astype(jnp.float32),
        taken_together(attn_rows[4].astype(jnp.bfloat16), "seq").astype(jnp.float32),
        taken_together(attn_rows[5].astype(jnp.bfloat16), "seq").astype(jnp.float32),
    )
    mlp_done = sum_packed((mlp_sum[0], mlp_sum[1], mlp_sum[2]), ("dp", "seq"), (1, 1, 0))
    return (
        outputs,
        grad_inputs,
        attn_done[0],
        attn_done[1],
        attn_done[2],
        attn_done[3],
        attn_done[4],
        attn_done[5],
        mlp_done[0],
        mlp_done[1],
        mlp_done[2],
    )


def solution(mesh):
    return jax.shard_map(
        local,
        mesh=mesh,
        in_specs=(
            P("dp", "seq", None),
            P("dp", None),
            P("dp"),
            P("dp", None),
            P("dp", None),
            P("dp", None),
            P("dp", None),
            P("dp"),
            P(None, ("dp", "seq")),
            P(None, ("dp", "seq")),
            P(("dp", "seq"), None),
            P("dp", "seq", None),
        ),
        out_specs=(
            P("dp", "seq", None),
            P("dp", "seq", None),
            P("dp"),
            P("dp", None),
            P("dp", None),
            P("dp", None),
            P("dp", None),
            P("dp"),
            P(None, ("dp", "seq")),
            P(None, ("dp", "seq")),
            P(("dp", "seq"), None),
        ),
        check_vma=False,
    )
```

profile of v0, /device:TPU:2, one launch (start us, length us, event | category | flops | bytes accessed | tf_op | source)
XLA Modules:
  0.0 1166.2 jit_solution(5728818144339149643)
XLA Ops:
  11.1 1.7 concatenate.71
  12.8 849.2 %while.34 = (s32[]{:T(128)}, f32[576]{0:T(1024)}, f32[576,576]{1,0:T(8,128)}, f32[576,192]{0,1:T(8,128)}, f32[576,192]{0,1:T(8,128)}, /*index=5*/f32[576,576]{1,...) while((s32[]{:T(128)}, f32[576]{0:T(1024)}, ...), condition=%wide.region_12.13_spmd.clone, body=%wide.region_0.12_spmd.clone.sunk | while | flops 3675668992 | bytes 317572832 | solution.py:320
  17.4 48.1 %all-gather.11.cloned.1.call-done = bf16[16,36,1538]{2,1,0:T(8,128)(2,1)} async-done(((bf16[1,36,1538]{2,1,0:T(8,128)(2,1)}), bf16[16,36,1538]{2,1,0:T(8,128)(2,1)}) %all-gather.11.cloned.1.call-update) | async-done | bytes 1771792 | tf_op jit(solution)/shard_map/while/body/eval_jaxpr/all_gather | solution.py:19
  65.5 2.8 reshape.572
  70.9 5.7 all-to-all-start
  79.8 9.2 all-to-all-done
  98.5 281.9 %all-gather.13.cloned.1.call-done = bf16[128,12,1728]{2,1,0:T(8,128)(2,1)} async-done(((bf16[1,12,1728]{2,1,0:T(8,128)(2,1)}), bf16[128,12,1728]{2,1,0:T(8,128)(2,1)}) %all-gather.13.cloned.1.call-update) | async-done | bytes 5308432 | tf_op jit(solution)/shard_map/while/body/eval_jaxpr/all_gather | solution.py:31
  380.4 10.2 reshape.573
  390.6 2.5 fusion.242
  393.1 2.3 fusion.241
  397.7 2.5 multiply_reduce_fusion.6
  414.1 1.7 copy-done.6
  416.9 6.5 all-to-all-start.1
  424.6 1.5 select_add_fusion.15
  427.3 2.4 select_add_fusion.18
  429.6 6.0 all-to-all-done.1
  443.8 46.3 %all-gather.11.cloned.1.call-done = bf16[16,36,1538]{2,1,0:T(8,128)(2,1)} async-done(((bf16[1,36,1538]{2,1,0:T(8,128)(2,1)}), bf16[16,36,1538]{2,1,0:T(8,128)(2,1)}) %all-gather.11.cloned.1.call-update) | async-done | bytes 1771792 | tf_op jit(solution)/shard_map/while/body/eval_jaxpr/all_gather | solution.py:19
  490.1 2.8 reshape.572
  495.5 5.7 all-to-all-start
  504.4 9.2 all-to-all-done
  523.1 279.4 %all-gather.13.cloned.1.call-done = bf16[128,12,1728]{2,1,0:T(8,128)(2,1)} async-done(((bf16[1,12,1728]{2,1,0:T(8,128)(2,1)}), bf16[128,12,1728]{2,1,0:T(8,128)(2,1)}) %all-gather.13.cloned.1.call-update) | async-done | bytes 5308432 | tf_op jit(solution)/shard_map/while/body/eval_jaxpr/all_gather | solution.py:31
  802.6 10.2 reshape.573
  812.8 2.5 fusion.242
  815.3 2.3 fusion.241
  819.8 2.5 multiply_reduce_fusion.6
  836.3 1.7 copy-done.6
  839.1 6.6 all-to-all-start.1
  846.8 2.9 select_add_fusion.15
  850.9 4.4 select_add_fusion.18
  855.2 2.6 all-to-all-done.1
  867.9 2.1 reshape_reshape.15
  872.5 4.9 dynamic-update-slice.1
  877.4 2.4 dynamic-update-slice.2
  879.8 2.4 dynamic-update-slice.3
  882.1 4.8 dynamic-update-slice.4
  888.3 1.6 pad.8
  889.9 1.8 reshape.532
  891.8 5.6 copy.188
  897.4 5.3 reshape.534
  902.7 6.3 copy.189
  909.0 5.2 reshape.535
  914.1 3.2 copy.190
  917.4 5.3 reshape.536
  922.7 6.1 copy.191
  928.8 5.0 reshape.537
  933.8 3.1 copy.192
  936.9 4.1 reshape_reshape.19
  941.0 3.0 copy.193
  944.0 11.2 pad_maximum_fusion.6
  955.2 11.6 copy.205
  966.7 9.2 pad.9.clone
  976.0 10.9 reshape.538
  987.7 8.3 all_to_all.54
  996.6 4.7 all-to-all-start.7
  1002.3 3.7 all-to-all-done.7
  1006.6 4.7 all-to-all-start.4
  1011.5 5.9 all-to-all-done.4
  1018.0 4.9 all-to-all-start.5
  1023.9 4.8 all-to-all-done.5
  1029.5 4.4 all-to-all-start.3
  1035.1 6.9 all-to-all-done.3
  1042.8 4.7 all-to-all-start.6
  1049.7 4.6 all-to-all-done.6
  1055.2 99.7 %all-reduce.6.cloned.1.call-done = f32[21504,128]{1,0:T(8,128)} async-done(((f32[21504,128]{1,0:T(8,128)}), f32[21504,128]{1,0:T(8,128)}) %all-reduce.6.cloned.1.call-update) | async-done | bytes 11010064
  (352 shorter events, 112.0 us)
Async XLA Ops:
  12.8 56.1 %copy-start.8 = (bf16[2,128,576]{1,2,0:T(8,128)(2,1)S(1)}, bf16[2,128,576]{1,2,0:T(8,128)(2,1)}, u32[]{:S(2)}) copy-start(bf16[2,128,576]{1,2,0:T(8,128)(2,1)} %get-tuple-element.881) | copy-start | bytes 884740 | tf_op jit(solution)/shard_map/while
  12.8 52.7 %all-gather.11.cloned.1.call-start = ((), (), s32[]{:S(2)}) async-start(), calls=%async_computation.11 | async-start | bytes 2263040 | tf_op jit(solution)/shard_map/while/body/eval_jaxpr/all_gather | solution.py:19
  13.5 366.9 %all-gather.13.cloned.1.call-start = ((), (), s32[]{:S(2)}) async-start(), calls=%async_computation.12 | async-start | bytes 7397376 | tf_op jit(solution)/shard_map/while/body/eval_jaxpr/all_gather | solution.py:31
  70.9 18.1 %all-to-all-start = ((bf16[8,128,384]{1,2,0:T(8,128)(2,1)}), bf16[8,128,384]{1,2,0:T(8,128)(2,1)}, u32[]{:S(2)}, u32[]{:S(2)}) async-start(bf16[8,128,384]{1,2,0:T(8,128)(2,1)} %broadcast_in_dim.175), calls=%async_computation | async-start | bytes 1572864 | tf_op jit(solution)/shard_map/while/body/eval_jaxpr/all_to_all | solution.py:49
  79.8 15.3 %copy-start.24 = (bf16[128,9,32]{0,2,1:T(8,128)(2,1)}, bf16[128,9,32]{0,2,1:T(8,128)(2,1)S(1)}, u32[]{:S(2)}) copy-start(bf16[128,9,32]{0,2,1:T(8,128)(2,1)S(1)} %get-tuple-element.803) | copy-start | bytes 221188 | tf_op jit(solution)/shard_map/while
  94.2 1.9 copy-start.15
  95.1 2.3 copy-start
  98.3 299.3 %copy-start.17 = (f32[128,576]{0,1:T(8,128)}, f32[128,576]{0,1:T(8,128)S(1)}, u32[]{:S(2)}) copy-start(f32[128,576]{0,1:T(8,128)S(1)} %get-tuple-element.808) | copy-start | bytes 884740 | tf_op jit(solution)/shard_map/while
  98.5 313.2 %copy-start.9 = (bf16[128,576]{0,1:T(8,128)(2,1)}, bf16[128,576]{0,1:T(8,128)(2,1)S(1)}, u32[]{:S(2)}) copy-start(bf16[128,576]{0,1:T(8,128)(2,1)S(1)} %multiply_convert_fusion.6) | copy-start | bytes 442372 | tf_op jit(solution)/shard_map/while
  390.6 4.9 copy-start.1
  395.4 6.3 slice-start
  396.7 4.5 copy-start.26
  396.7 3.4 copy-start.23
  396.7 5.0 slice-start.1
  407.0 1.9 copy-start.29
  407.9 2.8 copy-start.2
  410.7 2.3 copy-start.5
  411.7 2.4 copy-start.3
  416.0 10.1 copy-start.33
  416.9 18.7 %all-to-all-start.1 = ((bf16[8,128,384]{1,2,0:T(8,128)(2,1)}), bf16[8,128,384]{1,2,0:T(8,128)(2,1)S(1)}, u32[]{:S(2)}, u32[]{:S(2)}) async-start(bf16[8,128,384]{1,2,0:T(8,128)(2,1)} %pad_maximum_fusion.14), calls=%async_computation.1 | async-start | bytes 1572864 | tf_op jit(solution)/shard_map/while/body/eval_jaxpr/all_to_all | solution.py:64
  423.5 3.8 copy-start.10
  423.5 3.8 copy-start.27
  429.6 8.9 copy-start.31
  435.6 1.9 copy-start.21
  435.6 2.4 copy-start.19
  435.6 2.9 copy-start.34
  439.5 54.0 %copy-start.8 = (bf16[2,128,576]{1,2,0:T(8,128)(2,1)S(1)}, bf16[2,128,576]{1,2,0:T(8,128)(2,1)}, u32[]{:S(2)}) copy-start(bf16[2,128,576]{1,2,0:T(8,128)(2,1)} %get-tuple-element.881) | copy-start | bytes 884740 | tf_op jit(solution)/shard_map/while
  439.5 50.7 %all-gather.11.cloned.1.call-start = ((), (), s32[]{:S(2)}) async-start(), calls=%async_computation.11 | async-start | bytes 2263040 | tf_op jit(solution)/shard_map/while/body/eval_jaxpr/all_gather | solution.py:19
  440.2 362.4 %all-gather.13.cloned.1.call-start = ((), (), s32[]{:S(2)}) async-start(), calls=%async_computation.12 | async-start | bytes 7397376 | tf_op jit(solution)/shard_map/while/body/eval_jaxpr/all_gather | solution.py:31
  495.5 18.1 %all-to-all-start = ((bf16[8,128,384]{1,2,0:T(8,128)(2,1)}), bf16[8,128,384]{1,2,0:T(8,128)(2,1)}, u32[]{:S(2)}, u32[]{:S(2)}) async-start(bf16[8,128,384]{1,2,0:T(8,128)(2,1)} %broadcast_in_dim.175), calls=%async_computation | async-start | bytes 1572864 | tf_op jit(solution)/shard_map/while/body/eval_jaxpr/all_to_all | solution.py:49
  504.4 15.3 %copy-start.24 = (bf16[128,9,32]{0,2,1:T(8,128)(2,1)}, bf16[128,9,32]{0,2,1:T(8,128)(2,1)S(1)}, u32[]{:S(2)}) copy-start(bf16[128,9,32]{0,2,1:T(8,128)(2,1)S(1)} %get-tuple-element.803) | copy-start | bytes 221188 | tf_op jit(solution)/shard_map/while
  518.8 1.9 copy-start.15
  519.7 2.3 copy-start
  522.9 296.9 %copy-start.17 = (f32[128,576]{0,1:T(8,128)}, f32[128,576]{0,1:T(8,128)S(1)}, u32[]{:S(2)}) copy-start(f32[128,576]{0,1:T(8,128)S(1)} %get-tuple-element.808) | copy-start | bytes 884740 | tf_op jit(solution)/shard_map/while
  523.1 310.7 %copy-start.9 = (bf16[128,576]{0,1:T(8,128)(2,1)}, bf16[128,576]{0,1:T(8,128)(2,1)S(1)}, u32[]{:S(2)}) copy-start(bf16[128,576]{0,1:T(8,128)(2,1)S(1)} %multiply_convert_fusion.6) | copy-start | bytes 442372 | tf_op jit(solution)/shard_map/while
  812.8 4.9 copy-start.1
  817.6 6.3 slice-start
  818.9 4.5 copy-start.26
  818.9 3.4 copy-start.23
  818.9 5.0 slice-start.1
  829.2 1.9 copy-start.29
  830.1 2.8 copy-start.2
  832.9 2.3 copy-start.5
  833.8 2.4 copy-start.3
  838.2 11.6 copy-start.33
  839.1 18.7 %all-to-all-start.1 = ((bf16[8,128,384]{1,2,0:T(8,128)(2,1)}), bf16[8,128,384]{1,2,0:T(8,128)(2,1)S(1)}, u32[]{:S(2)}, u32[]{:S(2)}) async-start(bf16[8,128,384]{1,2,0:T(8,128)(2,1)} %pad_maximum_fusion.14), calls=%async_computation.1 | async-start | bytes 1572864 | tf_op jit(solution)/shard_map/while/body/eval_jaxpr/all_to_all | solution.py:64
  845.7 5.2 copy-start.10
  845.7 5.2 copy-start.27
  855.2 5.5 copy-start.31
  857.9 1.9 copy-start.21
  857.9 2.4 copy-start.19
  857.9 2.9 copy-start.34
  862.0 5.0 copy-start.14
  862.0 124.9 %reduce-scatter.4.cloned.1.call-start = ((), (), s32[]{:S(2)}) async-start(), calls=%async_computation.10 | async-start | bytes 1914880
  863.1 7.0 copy-start.13
  867.9 9.4 copy-start.30
  891.8 263.2 %all-reduce.6.cloned.1.call-start = ((), (), s32[]{:S(2)}) async-start(), calls=%async_computation.9 | async-start | bytes 22020096
  909.0 5.2 copy-start.7
  928.8 5.0 copy-start.4
  996.6 9.3 all-to-all-start.7
  1006.6 10.7 all-to-all-start.4
  1018.0 10.7 all-to-all-start.5
  1029.5 12.4 %all-to-all-start.3 = ((bf16[8,36,576]{2,1,0:T(8,128)(2,1)}), bf16[8,36,576]{2,1,0:T(8,128)(2,1)S(1)}, u32[]{:S(2)}, u32[]{:S(2)}) async-start(bf16[8,36,576]{2,1,0:T(8,128)(2,1)} %broadcast_in_dim.123), calls=%async_computation.3 | async-start | bytes 819200 | tf_op jit(solution)/shard_map/all_to_all | solution.py:49
  1042.8 11.6 all-to-all-start.6
  (26 other events, 29.0 us)
Sparse Core Ops, SparseCore 0:
  16.3 49.1 all-gather.10
  67.9 312.4 all-gather.12
  442.9 47.1 all-gather.10
  492.4 310.1 all-gather.12
  987.1 167.8 all-reduce.5
Sparse Core Ops, SparseCore 1:
  891.8 70.4 reduce-scatter.3
where the time goes:
time: 1190 us; the launch traced here: 1170 us
  waiting for transfers between devices  811 us (68%)
  local copies, waits for them, and re-layouts  182 us (15%)
  matrix products  63.6 us (5%)
  starting transfers between devices  48.1 us (4%)
  other arithmetic  35.2 us (3%)
  between operations  15.8 us (1%)
    all_gather x2, waiting for transfers between devices, gather_turned(): whole = lax.all_gather(both, axis, axis=0, tiled=True)  561 us
    unnamed x4, waiting for transfers between devices  99.8 us
    all_gather x2, waiting for transfers between devices, in_one_piece(): whole, at, outs = (lax.all_gather(both, axis, axis=dim, tiled=True), 0, [])  94.4 us
    all_to_all x7, waiting for transfers between devices, copy_for_each(): lax.all_to_all(jnp.broadcast_to(x[None], (length, *x.shape)), axis, 0, 0,...  44.2 us
    while x148, local copies, waits for them, and re-layouts  36.5 us
    all_to_all x7, starting transfers between devices, copy_for_each(): lax.all_to_all(jnp.broadcast_to(x[None], (length, *x.shape)), axis, 0, 0,...  34.8 us
    unnamed x18, local copies, waits for them, and re-layouts  28.9 us
  transfers between devices with their start and end apart: 15, of which 14 were waited for; matrix products, arithmetic and copies ran while one was open for 14% of the time, Pallas kernels for 0%

commit v1 on v0

v1 whole, which is shorter than its diff:
```python
import functools

import jax
import jax.numpy as jnp
from jax import lax
from jax.experimental import pallas as pl
from jax.experimental.pallas import tpu as pltpu
from jax.sharding import PartitionSpec as P

MESH = pl.DeviceIdType.MESH
F32 = jnp.float32
BF16 = jnp.bfloat16

D = 576
FF = 1536
QUERY_HEADS = 9
KV_HEADS = 3
HEAD_WIDTH = 64
ROPE_BASE = 100000.0
NORM_EPS = 1e-05
MASKED = -1e30

ROWS = 36
PAD = 48
BLOCKS = 16
DP_ROWS = BLOCKS * PAD
ORDERS = (("x", "y", "z"), ("y", "z", "x"), ("z", "x", "y"))


def dot_nn(a, b):
    return lax.dot_general(a, b, (((1,), (0,)), ((), ())), preferred_element_type=F32)


def dot_nt(a, b):
    return lax.dot_general(a, b, (((1,), (1,)), ((), ())), preferred_element_type=F32)


def dot_tn(a, b):
    return lax.dot_general(a, b, (((0,), (0,)), ((), ())), preferred_element_type=F32)


def iota(shape, dim):
    return lax.broadcasted_iota(jnp.int32, shape, dim)


def one_hot(cond):
    return jnp.where(cond, 1.0, 0.0).astype(BF16)


class Place:
    def __init__(self):
        self.dp = lax.axis_index("dp")
        self.seq = lax.axis_index("seq")
        self.z = self.dp // 4
        self.x_hi = (self.dp // 2) % 2
        self.core = self.dp % 2
        self.y = self.seq // 2
        self.x_lo = self.seq % 2
        self.x = 2 * self.x_hi + self.x_lo

    def at(self, x, y, z, core):
        return (z * 4 + (x // 2) * 2 + core, y * 2 + x % 2)

    def coordinate(self, axis):
        return {"x": self.x, "y": self.y, "z": self.z}[axis]

    def ring(self, axis, step):
        here = {"x": self.x, "y": self.y, "z": self.z}
        here[axis] = (here[axis] + step + 4) % 4
        return self.at(here["x"], here["y"], here["z"], self.core)

    def other_core(self):
        return (self.dp + 1 - 2 * self.core, self.seq)

    def group(self, dz, dx):
        z = (self.z + dz + 4) % 4
        x_hi = (self.x_hi + dx) % 2
        index = z * 2 + x_hi
        return (index * 2 + self.core, self.seq), index

    def rank(self, step):
        return (self.dp, (self.seq + step + 8) % 8)


class Net:
    def __init__(self, send, recv):
        self.send, self.recv, self.used = send, recv, 0
        self.unsent = []

    def new(self):
        self.used += 1
        return self.used - 1

    def copy(self, slot, src, dst, device):
        return pltpu.make_async_remote_copy(
            src_ref=src,
            dst_ref=dst,
            send_sem=self.send.at[slot],
            recv_sem=self.recv.at[slot],
            device_id=device,
            device_id_type=MESH,
        )

    def start(self, slot, src, dst, device):
        copy = self.copy(slot, src, dst, device)
        copy.start()
        self.unsent.append(copy)

    def arrived(self, slot, dst, device):
        self.copy(slot, dst, dst, device).wait_recv()

    def finish(self):
        for copy in self.unsent:
            copy.wait_send()


GROUP_STEPS = [(dz, dx) for dz in range(4) for dx in range(2) if (dz, dx) != (0, 0)]


class Summed:
    def __init__(self, net, place, refs):
        self.net, self.place = net, place
        self.mine, self.from_core, self.chip, self.from_group, self.one, self.from_rank = refs
        self.core_slot = net.new()
        self.group_slots = [net.new() for _ in GROUP_STEPS]
        self.rank_slots = [net.new() for _ in range(7)]

    def begin(self):
        place = self.place
        self.net.start(
            self.core_slot, self.mine.at[1 - place.core], self.from_core, place.other_core()
        )

    def over_group(self):
        place, net = self.place, self.net
        net.arrived(self.core_slot, self.from_core, place.other_core())
        self.chip[...] = (
            self.mine[place.core].astype(F32) + self.from_core[...].astype(F32)
        ).astype(BF16)
        for k, (dz, dx) in enumerate(GROUP_STEPS):
            device, index = place.group(dz, dx)
            net.start(self.group_slots[k], self.chip.at[index], self.from_group.at[k], device)

    def over_ranks(self):
        place, net = self.place, self.net
        for k, (dz, dx) in enumerate(GROUP_STEPS):
            device, _ = place.group(-dz, dx)
            net.arrived(self.group_slots[k], self.from_group.at[k], device)
        total = self.chip[place.z * 2 + place.x_hi].astype(F32)
        for k in range(7):
            total += self.from_group[k].astype(F32)
        self.one[...] = total.astype(BF16)
        for k in range(7):
            net.start(self.rank_slots[k], self.one, self.from_rank.at[k], place.rank(k + 1))

    def result(self):
        place, net = self.place, self.net
        for k in range(7):
            net.arrived(self.rank_slots[k], self.from_rank.at[k], place.rank(-k - 1))
        total = self.one[...].astype(F32)
        for k in range(7):
            total += self.from_rank[k].astype(F32)
        return total


def swap_halves(tile):
    first = (iota(tile.shape, 1) & 32) == 0
    return jnp.where(first, pltpu.roll(tile, 96, 1), pltpu.roll(tile, 32, 1))


def kernel(
    x_ref, seg_ref, a1_ref, a2_ref, wg_ref, wu_ref, wd_ref, dy_ref, freq_ref,
    out_ref, gx_ref, gna_ref, gq_ref, gk_ref, gv_ref, go_ref, gnm_ref, gg_ref, gu_ref, gd_ref,
    s,
):
    place = Place()
    net = Net(s["send"], s["recv"])
    rank = place.seq

    barrier = pltpu.get_barrier_semaphore()
    peers = [place.ring(axis, step) for axis in "xyz" for step in (1, 2, 3)]
    peers += [place.other_core()]
    peers += [place.group(dz, 1)[0] for dz in (1, 2, 3)]
    flipped = place.x + 1 - 2 * place.x_lo
    peers += [place.at(flipped, (place.y + dy) % 4, place.z, place.core) for dy in (1, 2, 3)]
    for peer in peers:
        pl.semaphore_signal(barrier, inc=1, device_id=peer, device_id_type=MESH)

    row, col = iota((16, 12), 0), iota((16, 12), 1)
    down = wd_ref[...]
    for p in range(3):
        tile = jnp.zeros((16, D), F32)
        for t, ref in enumerate((wg_ref, wu_ref, wd_ref)):
            pick = one_hot(((row >> 2) == t) & (col == 4 * p + (row & 3)))
            tile += dot_nn(pick, down) if t == 2 else dot_nt(pick, ref[...])
        s["tile"][p] = tile.astype(BF16)

    pl.semaphore_wait(barrier, len(peers))

    a1, a2 = s["a1"], s["a2"]
    other_dp = place.other_core()[0]
    a_slots = {}
    for name, ref, whole in (("a1", a1_ref, a1), ("a2", a2_ref, a2)):
        group_slots = [net.new() for _ in GROUP_STEPS]
        core_slots = [net.new() for _ in range(8)]
        a_slots[name] = (group_slots, core_slots)
    ff_slots = [[[net.new() for _ in range(3)] for _ in range(3)] for _ in range(3)]
    dy_slot, n2_slot, out_slot, dn2_slot = (net.new() for _ in range(4))

    def send_own(name, ref, whole):
        group_slots, core_slots = a_slots[name]
        for k, (dz, dx) in enumerate(GROUP_STEPS):
            net.start(group_slots[k], ref, whole.at[place.dp], place.group(dz, dx)[0])
        net.start(core_slots[7], ref, whole.at[place.dp], place.other_core())
        whole[place.dp] = ref[...]

    def pass_on(name, whole):
        group_slots, core_slots = a_slots[name]
        for k, (dz, dx) in enumerate(GROUP_STEPS):
            device, index = place.group(-dz, dx)
            block = whole.at[index * 2 + place.core]
            net.arrived(group_slots[k], block, device)
            net.start(core_slots[k], block, block, place.other_core())

    def have_all(name, whole):
        group_slots, core_slots = a_slots[name]
        for k, (dz, dx) in enumerate(GROUP_STEPS):
            _, index = place.group(-dz, dx)
            net.arrived(core_slots[k], whole.at[index * 2 + 1 - place.core], place.other_core())
        net.arrived(core_slots[7], whole.at[other_dp], place.other_core())

    send_own("a1", a1_ref, a1)
    for p, (one, _, _) in enumerate(ORDERS):
        mine = place.coordinate(one)
        s["first"][p, mine] = s["tile"][p]
        for d in (1, 2, 3):
            net.start(
                ff_slots[p][0][d - 1], s["tile"].at[p], s["first"].at[p, mine], place.ring(one, d)
            )
    send_own("a2", a2_ref, a2)
    s["dy"][0] = dy_ref[...].reshape(256, D)
    net.start(dy_slot, s["dy"].at[0], s["dy"].at[1], place.other_core())

    row = iota((D, DP_ROWS), 0).astype(F32)
    col = iota((D, DP_ROWS), 1).astype(F32)
    s["spread"][...] = one_hot(col - row == 12.0 * jnp.floor((row + 0.5) * (1.0 / ROWS)))
    lane = iota((128, 128), 1)
    for b in range(2):
        own = seg_ref[pl.ds(b, 1), pl.ds(pl.multiple_of(rank * 128, 128), 128)].astype(F32)
        own = jnp.transpose(jnp.broadcast_to(own, (128, 128)))
        earlier = jnp.zeros((128, 128), F32)
        for c in range(8):
            part = seg_ref[pl.ds(b, 1), pl.ds(128 * c, 128)].astype(F32)
            earlier += jnp.where(part < own, 1.0, 0.0)
        begin = jnp.sum(earlier, axis=1, keepdims=True)
        here = (iota((128, 1), 0) + rank * 128).astype(F32)
        angle = (here - begin) * freq_ref[...]
        s["cos"][pl.ds(128 * b, 128)] = jnp.cos(angle)
        sine = jnp.sin(angle)
        s["sin"][pl.ds(128 * b, 128)] = jnp.where((lane & 32) == 0, -sine, sine)
        for k in range(8):
            key = (lane + 128 * (rank - k)).astype(F32)
            s["bias"][b, :, pl.ds(128 * k, 128)] = jnp.where(
                (key >= begin) & (key <= here), 0.0, MASKED
            )
    x = x_ref[...].reshape(256, D)
    x32 = x.astype(F32)
    inv1 = lax.rsqrt(jnp.sum(x32 * x32, axis=1, keepdims=True) * (1.0 / D) + NORM_EPS)
    s["inv1"][...] = inv1
    s["unit1"][...] = dot_nn(x, s["spread"][...]) * inv1
    for k in range(1, 8):

        @pl.when(k > rank)
        def _(k=k):
            s["kv"][k] = jnp.zeros((2, 128, 384), BF16)

    row, col = iota((PAD, 64), 0), iota((PAD, 64), 1)
    pack = one_hot(col == (((row >> 2) & 3) << 4) + ((row >> 4) << 2) + (row & 3))
    row, col = iota((64, PAD), 0), iota((64, PAD), 1)
    unpack = one_hot(row == (((col >> 2) & 3) << 4) + ((col >> 4) << 2) + (col & 3))

    def ff_second():
        for p, (one, two, three) in enumerate(ORDERS):
            mine = place.coordinate(one)
            for d in (1, 2, 3):
                net.arrived(
                    ff_slots[p][0][d - 1], s["first"].at[p, (mine + 4 - d) % 4], place.ring(one, -d)
                )
            block = s["w"].at[p, place.coordinate(three), place.coordinate(two)]
            block[...] = dot_nn(pack, s["first"][p].reshape(64, D)).astype(BF16)
            for d in (1, 2, 3):
                net.start(ff_slots[p][1][d - 1], block, block, place.ring(two, d))

    def ff_third():
        for p, (_, two, three) in enumerate(ORDERS):
            mine, last = place.coordinate(two), place.coordinate(three)
            for d in (1, 2, 3):
                net.arrived(
                    ff_slots[p][1][d - 1], s["w"].at[p, last, (mine + 4 - d) % 4], place.ring(two, -d)
                )
            block = s["w"].at[p, last]
            for d in (1, 2, 3):
                net.start(ff_slots[p][2][d - 1], block, block, place.ring(three, d))

    def ff_have(p):
        three = ORDERS[p][2]
        last = place.coordinate(three)
        for d in (1, 2, 3):
            net.arrived(
                ff_slots[p][2][d - 1], s["w"].at[p, (last + 4 - d) % 4], place.ring(three, -d)
            )

    ff_second()
    pass_on("a1", a1)
    have_all("a1", a1)

    gains = jnp.transpose(a1[:, :, pl.ds(896, 128)].reshape(DP_ROWS, 128).astype(F32))
    gain1 = gains[64:65]
    s["gain1"][...] = gain1
    gain2 = dot_nt(gains[64:80].astype(BF16), s["spread"][...])[1:2]
    s["gain2"][...] = gain2
    s["n1"][...] = (s["unit1"][...] * gain1).astype(BF16)
    pre = dot_nn(s["n1"][...], a1[...].reshape(DP_ROWS, 1024))
    cos, sin = s["cos"][...], s["sin"][...]
    lane = iota((256, 128), 1)
    for t in range(8):
        tile = pre[:, 128 * t : 128 * t + 128]
        if t != 2:
            turned = tile * cos + swap_halves(tile) * sin
            tile = jnp.where(lane < 64, turned, tile) if t == 1 else turned
        if t < 3:
            s["kv"][0, :, :, pl.ds(128 * t, 128)] = tile.astype(BF16).reshape(2, 128, 128)
        else:
            tile = (tile * HEAD_WIDTH**-0.5).astype(BF16).reshape(2, 128, 128)
            s["q"][:, :, pl.ds(128 * t - 384, 128)] = tile

    kv_slots = [net.new() for _ in range(7)]
    kv_copies = []
    for k in range(1, 8):
        copy = net.copy(kv_slots[k - 1], s["kv"].at[0], s["kv"].at[k], place.rank(k))
        kv_copies.append(copy)
        pl.when(rank + k <= 7)(copy.start)
    ff_third()
    pass_on("a2", a2)
    for k in range(1, 8):
        pl.when(k <= rank)(
            functools.partial(net.arrived, kv_slots[k - 1], s["kv"].at[k], place.rank(-k))
        )

    def heads(value, group):
        return jnp.concatenate(
            [value[:, 64 * h : 64 * h + 64] for h in range(3 * group, 3 * group + 3)], axis=0
        )

    @pl.loop(0, 2)
    def _(b):
        bias = s["bias"][b]
        for g in range(3):
            query = heads(s["q"][b], g)
            keys = s["kv"][:, b, :, pl.ds(64 * g, 64)].reshape(1024, 64)
            values = s["kv"][:, b, :, pl.ds(192 + 64 * g, 64)].reshape(1024, 64)
            score = (dot_nt(query, keys).reshape(3, 128, 1024) + bias[None]).reshape(384, 1024)
            top = jnp.max(score, axis=1, keepdims=True)
            score = jnp.exp(score - top)
            inv = 1.0 / jnp.sum(score, axis=1, keepdims=True)
            weight = score.astype(BF16)
            s["attn"][b, g] = weight
            s["inv_sum"][b, g] = inv
            mixed = (dot_nn(weight, values) * inv).astype(BF16)
            for h in range(3):
                s["mixed"][b, :, pl.ds(64 * (3 * g + h), 64)] = mixed[128 * h : 128 * h + 128]

    have_all("a2", a2)
    w_out = a2[...].reshape(DP_ROWS, D)
    s["mixed_spread"][...] = dot_nn(s["mixed"][...].reshape(256, D), s["spread"][...]).astype(BF16)
    middle = x_ref[...].reshape(256, D).astype(F32) + dot_nn(s["mixed_spread"][...], w_out)
    s["middle"][...] = middle
    inv2 = lax.rsqrt(jnp.sum(middle * middle, axis=1, keepdims=True) * (1.0 / D) + NORM_EPS)
    s["inv2"][...] = inv2
    s["n2"][0] = (middle * inv2 * s["gain2"][...]).astype(BF16)
    net.start(n2_slot, s["n2"].at[0], s["n2"].at[1], place.other_core())
    net.arrived(dy_slot, s["dy"].at[1], place.other_core())
    net.arrived(n2_slot, s["n2"].at[1], place.other_core())

    rs_slots = [[[net.new() for _ in range(3)] for _ in range(3)] for _ in range(3)]
    normed, upper = s["n2"][...].reshape(512, D), s["dy"][...].reshape(512, D)
    for p in range(3):
        ff_have(p)
        w_gate, w_up, w_down = (
            s["w"][p, :, :, pl.ds(16 * t, 16), :].reshape(256, D) for t in range(3)
        )
        gate = dot_nt(normed, w_gate)
        up = dot_nt(normed, w_up)
        d_act = dot_nt(upper, w_down)
        sigmoid = 1.0 / (1.0 + jnp.exp(-gate))
        silu = gate * sigmoid
        act = (silu * up).astype(BF16)
        d_gate = (d_act * up * sigmoid * (1.0 + gate * (1.0 - sigmoid))).astype(BF16)
        d_up = (d_act * silu).astype(BF16)
        back = dot_nn(d_gate, w_gate) + dot_nn(d_up, w_up)
        ahead = dot_nn(act, w_down)
        if p == 0:
            s["dn2"][...] = back
            s["ahead"][...] = ahead
        else:
            s["dn2"][...] += back
            s["ahead"][...] += ahead
        for t, (left, right) in enumerate(((d_gate, normed), (d_up, normed), (act, upper))):
            s["g"][p, :, :, pl.ds(16 * t, 16), :] = (
                dot_tn(left, right).astype(BF16).reshape(4, 4, 16, D)
            )
        three = ORDERS[p][2]
        last = place.coordinate(three)
        for d in (1, 2, 3):
            net.start(
                rs_slots[p][0][d - 1],
                s["g"].at[p, (last + d) % 4],
                s["ra"].at[p, d - 1],
                place.ring(three, d),
            )
    s["dn2_out"][...] = s["dn2"][pl.ds(256, 256)].astype(BF16)
    net.start(dn2_slot, s["dn2_out"], s["dn2_in"], place.other_core())
    s["ahead_out"][...] = s["ahead"][pl.ds(256, 256)].astype(BF16)
    net.start(out_slot, s["ahead_out"], s["ahead_in"], place.other_core())

    def rs_second():
        for p, (_, two, three) in enumerate(ORDERS):
            for d in (1, 2, 3):
                net.arrived(rs_slots[p][0][d - 1], s["ra"].at[p, d - 1], place.ring(three, -d))
            total = s["g"][p, place.coordinate(three)].astype(F32)
            for d in range(3):
                total += s["ra"][p, d].astype(F32)
            s["s2"][p] = total.astype(BF16)
            mine = place.coordinate(two)
            for d in (1, 2, 3):
                net.start(
                    rs_slots[p][1][d - 1],
                    s["s2"].at[p, (mine + d) % 4],
                    s["rb"].at[p, d - 1],
                    place.ring(two, d),
                )

    def rs_third():
        for p, (one, two, _) in enumerate(ORDERS):
            for d in (1, 2, 3):
                net.arrived(rs_slots[p][1][d - 1], s["rb"].at[p, d - 1], place.ring(two, -d))
            total = s["s2"][p, place.coordinate(two)].astype(F32)
            for d in range(3):
                total += s["rb"][p, d].astype(F32)
            s["u"][p] = dot_nn(unpack, total.astype(BF16)).astype(BF16).reshape(4, 16, D)
            mine = place.coordinate(one)
            for d in (1, 2, 3):
                net.start(
                    rs_slots[p][2][d - 1],
                    s["u"].at[p, (mine + d) % 4],
                    s["rc"].at[p, d - 1],
                    place.ring(one, d),
                )

    def rs_result():
        for p, (one, _, _) in enumerate(ORDERS):
            for d in (1, 2, 3):
                net.arrived(rs_slots[p][2][d - 1], s["rc"].at[p, d - 1], place.ring(one, -d))
            total = s["u"][p, place.coordinate(one)].astype(F32)
            for d in range(3):
                total += s["rc"][p, d].astype(F32)
            s["f"][pl.ds(16 * p, 16)] = total

    net.arrived(dn2_slot, s["dn2_in"], place.other_core())
    d_normed = s["dn2"][pl.ds(0, 256)] + s["dn2_in"][...].astype(F32)
    middle, inv2 = s["middle"][...], s["inv2"][...]
    unit2 = middle * inv2
    scaled = d_normed * s["gain2"][...]
    inner = jnp.sum(scaled * unit2, axis=1, keepdims=True) * (1.0 / D)
    d_middle = s["dy"][0].astype(F32) + inv2 * (scaled - unit2 * inner)
    s["d_middle"][...] = d_middle
    g_gain2 = jnp.sum(d_normed * unit2, axis=0, keepdims=True)
    d_branch = d_middle.astype(BF16)
    w_out = a2[...].reshape(DP_ROWS, D)
    d_mixed = dot_nt(d_branch, w_out).astype(BF16)
    s["d_mixed"][...] = dot_nt(d_mixed, s["spread"][...]).astype(BF16).reshape(2, 128, D)
    out_sum = Summed(net, place, s["sum_out"])
    grad = dot_tn(s["mixed_spread"][...], d_branch).astype(BF16).reshape(8, 2, PAD, D)
    for c in range(2):
        s["sum_out"][0][c] = grad[:, c]
    out_sum.begin()

    dkv_slots = [[net.new() for _ in range(7)] for _ in range(2)]
    dkv_copies = []
    for b in range(2):
        for g in range(3):
            inv = s["inv_sum"][b, g]
            keys = s["kv"][:, b, :, pl.ds(64 * g, 64)].reshape(1024, 64)
            values = s["kv"][:, b, :, pl.ds(192 + 64 * g, 64)].reshape(1024, 64)
            query = heads(s["q"][b], g)
            d_out = (heads(s["d_mixed"][b], g).astype(F32) * inv).astype(BF16)
            inner = jnp.sum(
                d_out.astype(F32) * heads(s["mixed"][b], g).astype(F32), axis=1, keepdims=True
            )
            weight = s["attn"][b, g]
            d_score = (weight.astype(F32) * (dot_nt(d_out, values) - inner)).astype(BF16)
            d_query = dot_nn(d_score, keys) * HEAD_WIDTH**-0.5
            for h in range(3):
                s["dq"][b, :, pl.ds(64 * (3 * g + h), 64)] = d_query[128 * h : 128 * h + 128]
            d_keys = jnp.transpose(dot_tn(query, d_score)).astype(BF16)
            d_values = jnp.transpose(dot_tn(d_out, weight)).astype(BF16)
            s["dkv"][:, b, :, pl.ds(64 * g, 64)] = d_keys.reshape(8, 128, 64)
            s["dkv"][:, b, :, pl.ds(192 + 64 * g, 64)] = d_values.reshape(8, 128, 64)
        for k in range(1, 8):
            copy = net.copy(
                dkv_slots[b][k - 1], s["dkv"].at[k, b], s["dkv_in"].at[k, b], place.rank(-k)
            )
            dkv_copies.append((k, copy))
            pl.when(k <= rank)(copy.start)
        if b == 0:
            out_sum.over_group()
            rs_second()
    net.arrived(out_slot, s["ahead_in"], place.other_core())
    out = s["middle"][...] + s["ahead"][pl.ds(0, 256)] + s["ahead_in"][...].astype(F32)
    out_ref[...] = out.astype(BF16).reshape(2, 128, D)

    cos, sin = s["cos"][...], s["sin"][...]
    lane = iota((256, 128), 1)
    for t in range(5):
        if t < 4:
            tile = s["dq"][:, :, pl.ds(128 * t, 128)].reshape(256, 128)
        else:
            tile = s["dq"][:, :, pl.ds(512, 64)].reshape(256, 64)
            tile = jnp.concatenate([tile, jnp.zeros((256, 64), F32)], axis=1)
        tile = tile * cos - swap_halves(tile) * sin
        s["dqkv"][:, pl.ds(384 + 128 * t, 128)] = tile.astype(BF16)
    n1 = s["n1"][...]
    q_sum = Summed(net, place, s["sum_q"])
    grad = dot_tn(n1, s["dqkv"][:, pl.ds(384, 512)]).astype(BF16).reshape(8, 2, PAD, 512)
    for c in range(2):
        s["sum_q"][0][c] = grad[:, c]
    q_sum.begin()
    out_sum.over_ranks()
    rs_third()
    q_sum.over_group()

    for b in range(2):
        s["dkv_sum"][b] = s["dkv"][0, b].astype(F32)
    for k in range(1, 8):

        @pl.when(rank + k <= 7)
        def _(k=k):
            for b in range(2):
                net.arrived(dkv_slots[b][k - 1], s["dkv_in"].at[k, b], place.rank(k))
            s["dkv_sum"][...] += s["dkv_in"][k].astype(F32)

    for t in range(3):
        tile = s["dkv_sum"][:, :, pl.ds(128 * t, 128)].reshape(256, 128)
        if t < 2:
            turned = tile * cos - swap_halves(tile) * sin
            tile = jnp.where(lane < 64, turned, tile) if t == 1 else turned
        s["dqkv"][:, pl.ds(128 * t, 128)] = tile.astype(BF16)
    d_pre = s["dqkv"][...]
    d_normed = dot_nt(d_pre, a1[...].reshape(DP_ROWS, 1024))
    unit1 = s["unit1"][...]
    g_gain1 = jnp.sum(d_normed * unit1, axis=0, keepdims=True)
    spread = s["spread"][...]
    g_gain2 = dot_nn(jnp.broadcast_to(g_gain2, (16, D)).astype(BF16), spread)[0:1]
    row = iota((128, DP_ROWS), 0)
    g_gains = jnp.transpose(jnp.where(row == 64, g_gain1, jnp.where(row == 65, g_gain2, 0.0)))
    t_sum = Summed(net, place, s["sum_t"])
    grad = dot_tn(n1, d_pre[:, 0:384]).astype(BF16).reshape(8, 2, PAD, 384)
    rest = dot_tn(n1, d_pre[:, 896:1024]) + g_gains
    rest = rest.astype(BF16).reshape(8, 2, PAD, 128)
    for c in range(2):
        s["sum_t"][0][c, :, :, pl.ds(0, 384)] = grad[:, c]
        s["sum_t"][0][c, :, :, pl.ds(384, 128)] = rest[:, c]
    t_sum.begin()

    scaled = d_normed * s["gain1"][...]
    inner = jnp.sum(scaled * unit1, axis=1, keepdims=True) * (1.0 / D)
    d_in = s["inv1"][...] * (scaled - unit1 * inner)
    high = d_in.astype(BF16)
    low = (d_in - high.astype(F32)).astype(BF16)
    d_in = s["d_middle"][...] + dot_nt(high, spread) + dot_nt(low, spread)
    gx_ref[...] = d_in.astype(BF16).reshape(2, 128, D)

    t_sum.over_group()
    q_sum.over_ranks()
    rs_result()
    sums = s["f"][...]
    high = sums.astype(BF16)
    low = (sums - high.astype(F32)).astype(BF16)
    row, col = iota((PAD, 12), 0), iota((PAD, 12), 1)
    for t, ref in enumerate((gg_ref, gu_ref)):
        pick = one_hot(row == ((col >> 2) << 4) + 4 * t + (col & 3))
        ref[...] = dot_tn(high, pick) + dot_tn(low, pick)
    row, col = iota((12, PAD), 0), iota((12, PAD), 1)
    pick = one_hot(col == ((row >> 2) << 4) + 8 + (row & 3))
    gd_ref[...] = dot_nn(pick, high) + dot_nn(pick, low)
    go_ref[...] = out_sum.result()[0:ROWS]
    t_sum.over_ranks()
    total = q_sum.result()
    gq_ref[:, pl.ds(0, 512)] = total[0:ROWS]
    total = t_sum.result()
    gk_ref[...] = total[0:ROWS, 0:192]
    gv_ref[...] = total[0:ROWS, 192:384]
    gq_ref[:, pl.ds(512, 64)] = total[0:ROWS, 384:448]
    across = jnp.transpose(total[:, 384:512])
    gna_ref[...] = across[64:65, 0:ROWS]
    gnm_ref[...] = across[65:66, 0:ROWS]

    net.finish()
    for k, copy in enumerate(kv_copies, 1):
        pl.when(rank + k <= 7)(copy.wait_send)
    for k, copy in dkv_copies:
        pl.when(k <= rank)(copy.wait_send)


def sum_buffers(width):
    return [
        pltpu.VMEM((2, 8, PAD, width), BF16),
        pltpu.VMEM((8, PAD, width), BF16),
        pltpu.VMEM((8, PAD, width), BF16),
        pltpu.VMEM((7, PAD, width), BF16),
        pltpu.VMEM((PAD, width), BF16),
        pltpu.VMEM((7, PAD, width), BF16),
    ]


COPIES = 160

SCRATCH = {
    "send": pltpu.SemaphoreType.DMA((COPIES,)),
    "recv": pltpu.SemaphoreType.DMA((COPIES,)),
    "tile": pltpu.VMEM((3, 16, D), BF16),
    "first": pltpu.VMEM((3, 4, 16, D), BF16),
    "w": pltpu.VMEM((3, 4, 4, PAD, D), BF16),
    "a1": pltpu.VMEM((BLOCKS, PAD, 1024), BF16),
    "a2": pltpu.VMEM((BLOCKS, PAD, D), BF16),
    "spread": pltpu.VMEM((D, DP_ROWS), BF16),
    "cos": pltpu.VMEM((256, 128), F32),
    "sin": pltpu.VMEM((256, 128), F32),
    "bias": pltpu.VMEM((2, 128, 1024), F32),
    "inv1": pltpu.VMEM((256, 1), F32),
    "unit1": pltpu.VMEM((256, DP_ROWS), F32),
    "gain1": pltpu.VMEM((1, DP_ROWS), F32),
    "gain2": pltpu.VMEM((1, D), F32),
    "n1": pltpu.VMEM((256, DP_ROWS), BF16),
    "q": pltpu.VMEM((2, 128, 640), BF16),
    "kv": pltpu.VMEM((8, 2, 128, 384), BF16),
    "attn": pltpu.VMEM((2, 3, 384, 1024), BF16),
    "inv_sum": pltpu.VMEM((2, 3, 384, 1), F32),
    "mixed": pltpu.VMEM((2, 128, D), BF16),
    "mixed_spread": pltpu.VMEM((256, DP_ROWS), BF16),
    "middle": pltpu.VMEM((256, D), F32),
    "inv2": pltpu.VMEM((256, 1), F32),
    "n2": pltpu.VMEM((2, 256, D), BF16),
    "dy": pltpu.VMEM((2, 256, D), BF16),
    "dn2": pltpu.VMEM((512, D), F32),
    "ahead": pltpu.VMEM((512, D), F32),
    "dn2_out": pltpu.VMEM((256, D), BF16),
    "dn2_in": pltpu.VMEM((256, D), BF16),
    "ahead_out": pltpu.VMEM((256, D), BF16),
    "ahead_in": pltpu.VMEM((256, D), BF16),
    "d_middle": pltpu.VMEM((256, D), F32),
    "d_mixed": pltpu.VMEM((2, 128, D), BF16),
    "dq": pltpu.VMEM((2, 128, D), F32),
    "dkv": pltpu.VMEM((8, 2, 128, 384), BF16),
    "dkv_in": pltpu.VMEM((8, 2, 128, 384), BF16),
    "dkv_sum": pltpu.VMEM((2, 128, 384), F32),
    "dqkv": pltpu.VMEM((256, 1024), BF16),
    "g": pltpu.VMEM((3, 4, 4, PAD, D), BF16),
    "ra": pltpu.VMEM((3, 3, 4, PAD, D), BF16),
    "s2": pltpu.VMEM((3, 4, PAD, D), BF16),
    "rb": pltpu.VMEM((3, 3, PAD, D), BF16),
    "u": pltpu.VMEM((3, 4, 16, D), BF16),
    "rc": pltpu.VMEM((3, 3, 16, D), BF16),
    "f": pltpu.VMEM((PAD, D), F32),
    "sum_out": sum_buffers(D),
    "sum_q": sum_buffers(512),
    "sum_t": sum_buffers(512),
}


def local(
    inputs, segment_ids, norm_attn, w_query, w_key, w_value, w_out, norm_mlp, w_gate, w_up, w_down, cotangent,
):
    columns = [w_key, w_value, w_query, norm_attn[:, None], norm_mlp[:, None]]
    a1 = jnp.pad(jnp.concatenate(columns, axis=1), ((0, PAD - ROWS), (0, 62)))
    a2 = jnp.pad(w_out, ((0, PAD - ROWS), (0, 0)))
    half = HEAD_WIDTH // 2
    freq = ROPE_BASE ** (-(2.0 * jnp.arange(half, dtype=F32)) / HEAD_WIDTH)
    freq = jnp.tile(freq, 4)[None, :]
    shapes = [
        ((2, 128, D), BF16),
        ((2, 128, D), BF16),
        ((1, ROWS), F32),
        ((ROWS, 576), F32),
        ((ROWS, 192), F32),
        ((ROWS, 192), F32),
        ((ROWS, D), F32),
        ((1, ROWS), F32),
        ((D, 12), F32),
        ((D, 12), F32),
        ((12, D), F32),
    ]
    outs = pl.pallas_call(
        kernel,
        out_shape=[jax.ShapeDtypeStruct(shape, dtype) for shape, dtype in shapes],
        in_specs=[pl.BlockSpec(memory_space=pltpu.VMEM)] * 9,
        out_specs=[pl.BlockSpec(memory_space=pltpu.VMEM)] * len(shapes),
        scratch_shapes=[SCRATCH],
        compiler_params=pltpu.CompilerParams(
            collective_id=0, has_side_effects=True, vmem_limit_bytes=60 * 2**20
        ),
        name="layer",
    )(inputs, segment_ids, a1, a2, w_gate, w_up, w_down, cotangent, freq)
    outs = list(outs)
    outs[2], outs[7] = outs[2].reshape(ROWS), outs[7].reshape(ROWS)
    return tuple(outs)


def solution(mesh):
    rows, both = P("dp", None), ("dp", "seq")
    tokens = P("dp", "seq", None)
    weights = (P("dp"), rows, rows, rows, rows, P("dp"), P(None, both), P(None, both), P(both, None))
    return jax.shard_map(
        local,
        mesh=mesh,
        in_specs=(tokens, P("dp", None), *weights, tokens),
        out_specs=(tokens, tokens, *weights),
        check_vma=False,
    )
```

time: 1190 us -> 142 us (0.12); the launches traced: 1170 us -> 140 us
  waiting for transfers between devices: 811 us -> 0 us
  local copies, waits for them, and re-layouts: 182 us -> 15.9 us
  Pallas kernels: 0 us -> 123 us
  matrix products: 63.6 us -> 0 us
  starting transfers between devices: 48.1 us -> 0 us
  other arithmetic: 35.2 us -> 0.01 us
  between operations: 15.8 us -> 0.74 us
    all_gather x4 -> x0, waiting for transfers between devices: 656 us -> none  [the longest x2 561 us: gather_turned(): whole = lax.all_gather(both, axis, axis=0, tiled=True)]
    pallas_call x0 -> x1, Pallas kernels: none -> 123 us  [local(): pl.pallas_call(kernel, out_shape=[jax.ShapeDtypeStruct(shape, dtype) for...]
    unnamed x4 -> x0, waiting for transfers between devices: 99.8 us -> none
    dot_general x54 -> x0, matrix products: 63.6 us -> none  [the longest x14 18.4 us: dot_second(): lax.dot_general(left_side, right_side, (((1,), (1,)), ((), ())), preferre...]
    all_to_all x9 -> x0, waiting for transfers between devices: 52.7 us -> none  [the longest x7 44.2 us: copy_for_each(): lax.all_to_all(jnp.broadcast_to(x[None], (length, *x.shape)), axis, 0, 0,...]
    while x151 -> x0, local copies, waits for them, and re-layouts: 48.4 us -> none
    all_to_all x9 -> x0, starting transfers between devices: 48 us -> none  [the longest x7 34.8 us: copy_for_each(): lax.all_to_all(jnp.broadcast_to(x[None], (length, *x.shape)), axis, 0, 0,...]
    reshape x13 -> x0, local copies, waits for them, and re-layouts: 36.6 us -> none  [the longest x2 12.7 us: sum_packed(): jnp.pad(lines, ((0, 0), (0, rows * 128 - lines.shape[1]))).reshape(-1, 128)]
  transfers between devices with their start and end apart: 15 -> 0, of which waited for: 14 -> 0; matrix products, arithmetic and copies ran while one was open for 14% -> 0% of each run, Pallas kernels for 0% -> 0%
where the time goes in v1:
time: 142 us; the launch traced here: 140 us
  Pallas kernels  123 us (87%)
  local copies, waits for them, and re-layouts  15.9 us (11%)
    pallas_call x1, Pallas kernels, local(): pl.pallas_call(kernel, out_shape=[jax.ShapeDtypeStruct(shape, dtype) for...  123 us
    unnamed x49, local copies, waits for them, and re-layouts  12.2 us

profile of v1, /device:TPU:2, one launch (start us, length us, event | category | flops | bytes accessed | tf_op | source)
XLA Modules:
  0.0 139.8 jit_solution(3930371866657192700)
XLA Ops:
  0.6 0.0 copy-start.11
  0.7 0.6 broadcast_in_dim_tile.3.freq_ref
  1.3 0.0 copy-start.14
  1.3 0.8 copy.23
  2.1 0.0 copy-done.14
  2.1 0.1 copy.24
  2.2 0.0 copy-done.11
  2.2 0.0 copy-start.7
  2.2 0.0 copy-start.12
  2.2 0.9 concatenate.3
  3.1 0.0 copy-start.1
  3.1 0.7 pad.8.a1_ref
  3.8 0.0 copy-done.7
  3.8 0.6 pad.9.a2_ref
  4.4 0.0 copy-done.12
  4.4 0.0 copy-start.13
  4.4 0.8 copy.26.wg_ref
  5.2 0.0 copy-done.13
  5.2 0.8 copy.27.wu_ref
  6.1 0.0 copy-done.1
  6.1 0.0 copy-start.2
  6.1 0.9 copy.25.x_ref
  7.0 0.1 copy-done.2
  7.0 0.9 copy.28.dy_ref
  7.9 123.2 %layer.1 = (bf16[2,128,576]{2,1,0:T(8,128)(2,1)}, bf16[2,128,576]{2,1,0:T(8,128)(2,1)}, f32[1,36]{1,0:T(1,128)}, f32[36,576]{1,0:T(8,128)}, f32[36,192]{1,0:T(8,...) custom-call(bf16[2,128,576]{2,1,0:T(8,128)(2,1)} %copy.25.x_ref, ...), custom_call_target="tpu_custom_call" | custom-call | tf_op jit(solution)/shard_map/layer/pallas_call | solution.py:703
  131.1 0.0 copy-start.4
  131.1 0.0 copy-start.3
  131.1 1.9 %copy.29 = bf16[2,128,576]{1,2,0:T(8,128)(2,1)} copy(bf16[2,128,576]{2,1,0:T(8,128)(2,1)} %get-tuple-element.33) | data formatting | bytes 589824
  133.0 0.0 copy-done.4
  133.0 0.0 copy-start
  133.0 0.8 copy.31
  133.8 0.0 copy-done.3
  133.8 0.8 copy.32
  134.6 0.0 copy-done
  134.6 0.0 copy-start.16
  134.6 0.0 copy-start.6
  134.6 0.9 copy.30
  135.5 0.0 copy-done.16
  135.5 0.5 copy.40
  136.0 0.0 copy-done.6
  136.0 0.0 copy-start.10
  136.0 0.0 copy-start.9
  136.0 0.6 copy.41
  136.6 0.1 copy-done.10
  136.8 0.0 copy-start.5
  136.8 0.6 copy.42
  137.4 0.0 copy-done.9
  137.4 0.6 copy.43
  138.0 0.0 copy-done.5
  138.0 0.0 copy-start.15
  138.0 0.0 copy-start.8
  138.0 0.6 copy.44
  138.6 0.0 copy-done.15
  138.7 0.5 copy.45
  139.2 0.0 copy-done.8
  139.2 0.6 copy.46
  (2 shorter events, 0.0 us)
Async XLA Ops:
  0.6 1.5 %copy-start.11 = (bf16[36,192]{1,0:T(8,128)(2,1)S(1)}, bf16[36,192]{1,0:T(8,128)(2,1)}, u32[]{:S(2)}) copy-start(bf16[36,192]{1,0:T(8,128)(2,1)} %param.16) | copy-start | bytes 41476
  1.3 0.8 copy-start.14
  2.2 1.6 %copy-start.7 = (bf16[36,576]{1,0:T(8,128)(2,1)S(1)}, bf16[36,576]{1,0:T(8,128)(2,1)}, u32[]{:S(2)}) copy-start(bf16[36,576]{1,0:T(8,128)(2,1)} %param.18) | copy-start | bytes 124420
  2.2 2.3 %copy-start.12 = (bf16[576,12]{0,1:T(8,128)(2,1)S(1)}, bf16[576,12]{0,1:T(8,128)(2,1)}, u32[]{:S(2)}) copy-start(bf16[576,12]{0,1:T(8,128)(2,1)} %param.20) | copy-start | bytes 41476
  3.1 2.9 %copy-start.1 = (bf16[2,128,576]{1,2,0:T(8,128)(2,1)S(1)}, bf16[2,128,576]{1,2,0:T(8,128)(2,1)}, u32[]{:S(2)}) copy-start(bf16[2,128,576]{1,2,0:T(8,128)(2,1)} %param.12) | copy-start | bytes 884740
  4.4 0.8 copy-start.13
  6.1 1.0 copy-start.2
  131.1 1.9 %copy-start.4 = (f32[576,12]{1,0:T(8,128)S(1)}, f32[576,12]{1,0:T(8,128)}, u32[]{:S(2)}) copy-start(f32[576,12]{1,0:T(8,128)} %get-tuple-element.41) | copy-start | bytes 82948
  131.1 2.7 %copy-start.3 = (f32[576,12]{1,0:T(8,128)S(1)}, f32[576,12]{1,0:T(8,128)}, u32[]{:S(2)}) copy-start(f32[576,12]{1,0:T(8,128)} %get-tuple-element.42) | copy-start | bytes 82948
  133.0 1.5 %copy-start = (bf16[2,128,576]{2,1,0:T(8,128)(2,1)S(1)}, bf16[2,128,576]{2,1,0:T(8,128)(2,1)}, u32[]{:S(2)}) copy-start(bf16[2,128,576]{2,1,0:T(8,128)(2,1)} %get-tuple-element.34) | copy-start | bytes 884740
  134.6 0.9 copy-start.16
  134.6 1.4 %copy-start.6 = (f32[36,576]{1,0:T(8,128)S(1)}, f32[36,576]{1,0:T(8,128)}, u32[]{:S(2)}) copy-start(f32[36,576]{1,0:T(8,128)} %get-tuple-element.58) | copy-start | bytes 248836
  136.0 0.8 copy-start.10
  136.0 1.4 %copy-start.9 = (f32[36,192]{1,0:T(8,128)S(1)}, f32[36,192]{1,0:T(8,128)}, u32[]{:S(2)}) copy-start(f32[36,192]{1,0:T(8,128)} %get-tuple-element.60) | copy-start | bytes 82948
  136.8 1.2 copy-start.5
  138.0 0.6 copy-start.15
  138.0 1.2 copy-start.8

commit v2 on v1

--- a/solution.py
+++ b/solution.py
@@ -2,6 +2,7 @@
 
 import jax
 import jax.numpy as jnp
+import numpy as np
 from jax import lax
 from jax.experimental import pallas as pl
 from jax.experimental.pallas import tpu as pltpu
@@ -25,6 +26,7 @@
 BLOCKS = 16
 DP_ROWS = BLOCKS * PAD
 ORDERS = (("x", "y", "z"), ("y", "z", "x"), ("z", "x", "y"))
+BACK = (("z", "y"), ("z", "x"), ("x", "y"))
 
 
 def dot_nn(a, b):
@@ -74,9 +76,11 @@
 
     def group(self, dz, dx):
         z = (self.z + dz + 4) % 4
-        x_hi = (self.x_hi + dx) % 2
-        index = z * 2 + x_hi
-        return (index * 2 + self.core, self.seq), index
+        x = 3 - self.x if dx else self.x
+        return self.at(x, self.y, z, self.core), z * 2 + x // 2
+
+    def pair(self):
+        return self.at(self.x + 1 - 2 * self.x_lo, self.y, self.z, self.core)
 
     def rank(self, step):
         return (self.dp, (self.seq + step + 8) % 8)
@@ -85,7 +89,7 @@
 class Net:
     def __init__(self, send, recv):
         self.send, self.recv, self.used = send, recv, 0
-        self.unsent = []
+        self.unsent, self.maybe_unsent = [], []
 
     def new(self):
         self.used += 1
@@ -109,9 +113,19 @@
     def arrived(self, slot, dst, device):
         self.copy(slot, dst, dst, device).wait_recv()
 
+    def start_if(self, wanted, slot, src, dst, device):
+        copy = self.copy(slot, src, dst, device)
+        pl.when(wanted)(copy.start)
+        self.maybe_unsent.append((wanted, copy))
+
+    def arrived_if(self, wanted, slot, dst, device):
+        pl.when(wanted)(functools.partial(self.arrived, slot, dst, device))
+
     def finish(self):
         for copy in self.unsent:
             copy.wait_send()
+        for wanted, copy in self.maybe_unsent:
+            pl.when(wanted)(copy.wait_send)
 
 
 GROUP_STEPS = [(dz, dx) for dz in range(4) for dx in range(2) if (dz, dx) != (0, 0)]
@@ -124,6 +138,12 @@
         self.core_slot = net.new()
         self.group_slots = [net.new() for _ in GROUP_STEPS]
         self.rank_slots = [net.new() for _ in range(7)]
+
+    def fill(self, first, value):
+        width = value.shape[1]
+        value = value.astype(BF16).reshape(8, 2, PAD, width)
+        for c in range(2):
+            self.mine[c, :, :, pl.ds(first, width)] = value[:, c]
 
     def begin(self):
         place = self.place
@@ -163,13 +183,124 @@
         return total
 
 
+class SplitSummed:
+    def __init__(self, net, place, refs):
+        self.net, self.place = net, place
+        (
+            self.mine, self.from_core, self.chip, self.from_y, self.part, self.from_group, self.one, self.from_pair,
+            self.whole,
+        ) = refs
+        self.core_slot, self.pair_slot = net.new(), net.new()
+        self.y_slots = [net.new() for _ in range(3)]
+        self.group_slots = [net.new() for _ in GROUP_STEPS]
+        self.back_slots = [net.new() for _ in range(3)]
+
+    def fill(self, value):
+        value = value.astype(BF16)
+        for t in range(4):
+            tile = value[:, 128 * t : 128 * t + 128].reshape(8, 2, PAD, 128)
+            for c in range(2):
+                self.mine[c, t] = tile[:, c]
+
+    def begin(self):
+        place = self.place
+        self.net.start(
+            self.core_slot, self.mine.at[1 - place.core], self.from_core, place.other_core()
+        )
+
+    def over_y(self):
+        place, net = self.place, self.net
+        net.arrived(self.core_slot, self.from_core, place.other_core())
+        self.chip[...] = (
+            self.mine[place.core].astype(F32) + self.from_core[...].astype(F32)
+        ).astype(BF16)
+        for d in (1, 2, 3):
+            net.start(
+                self.y_slots[d - 1],
+                self.chip.at[(place.y + d) % 4],
+                self.from_y.at[d - 1],
+                place.ring("y", d),
+            )
+
+    def over_group(self):
+        place, net = self.place, self.net
+        for d in (1, 2, 3):
+            net.arrived(self.y_slots[d - 1], self.from_y.at[d - 1], place.ring("y", -d))
+        total = self.chip[place.y].astype(F32)
+        for d in range(3):
+            total += self.from_y[d].astype(F32)
+        self.part[...] = total.astype(BF16)
+        for k, (dz, dx) in enumerate(GROUP_STEPS):
+            device, index = place.group(dz, dx)
+            net.start(self.group_slots[k], self.part.at[index], self.from_group.at[k], device)
+
+    def over_pair(self):
+        place, net = self.place, self.net
+        for k, (dz, dx) in enumerate(GROUP_STEPS):
+            device, _ = place.group(-dz, dx)
+            net.arrived(self.group_slots[k], self.from_group.at[k], device)
+        total = self.part[place.z * 2 + place.x_hi].astype(F32)
+        for k in range(7):
+            total += self.from_group[k].astype(F32)
+        self.one[...] = total.astype(BF16)
+        net.start(self.pair_slot, self.one, self.from_pair, place.pair())
+
+    def back(self):
+        place, net = self.place, self.net
+        net.arrived(self.pair_slot, self.from_pair, place.pair())
+        total = self.one[...].astype(F32) + self.from_pair[...].astype(F32)
+        self.whole[place.y] = total.astype(BF16)
+        for d in (1, 2, 3):
+            tile = self.whole.at[place.y]
+            net.start(self.back_slots[d - 1], tile, tile, place.ring("y", d))
+
+    def result(self, ref):
+        place, net = self.place, self.net
+        for d in (1, 2, 3):
+            net.arrived(
+                self.back_slots[d - 1], self.whole.at[(place.y + 4 - d) % 4], place.ring("y", -d)
+            )
+        for t in range(4):
+            ref[:, pl.ds(128 * t, 128)] = self.whole[t, pl.ds(0, ROWS)].astype(F32)
+
+
+class Gathered:
+    def __init__(self, net, place, whole):
+        self.net, self.place, self.whole = net, place, whole
+        self.group_slots = [net.new() for _ in GROUP_STEPS]
+        self.core_slots = [net.new() for _ in range(8)]
+
+    def begin(self):
+        place, net = self.place, self.net
+        block = self.whole.at[place.dp]
+        for k, (dz, dx) in enumerate(GROUP_STEPS):
+            net.start(self.group_slots[k], block, block, place.group(dz, dx)[0])
+        net.start(self.core_slots[7], block, block, place.other_core())
+
+    def pass_on(self):
+        place, net = self.place, self.net
+        for k, (dz, dx) in enumerate(GROUP_STEPS):
+            device, index = place.group(-dz, dx)
+            block = self.whole.at[index * 2 + place.core]
+            net.arrived(self.group_slots[k], block, device)
+            net.start(self.core_slots[k], block, block, place.other_core())
+
+    def finish(self):
+        place, net = self.place, self.net
+        for k, (dz, dx) in enumerate(GROUP_STEPS):
+            _, index = place.group(-dz, dx)
+            block = self.whole.at[index * 2 + 1 - place.core]
+            net.arrived(self.core_slots[k], block, place.other_core())
+        net.arrived(self.core_slots[7], self.whole.at[place.other_core()[0]], place.other_core())
+
+
 def swap_halves(tile):
     first = (iota(tile.shape, 1) & 32) == 0
     return jnp.where(first, pltpu.roll(tile, 96, 1), pltpu.roll(tile, 32, 1))
 
 
 def kernel(
-    x_ref, seg_ref, a1_ref, a2_ref, wg_ref, wu_ref, wd_ref, dy_ref, freq_ref,
+    x_ref, seg_ref, na_ref, wq_ref, wk_ref, wv_ref, wo_ref, nm_ref, wg_ref, wu_ref, wd_ref, dy_ref, freq_ref,
     out_ref, gx_ref, gna_ref, gq_ref, gk_ref, gv_ref, go_ref, gnm_ref, gg_ref, gu_ref, gd_ref,
     s,
 ):
@@ -186,50 +317,32 @@
     for peer in peers:
         pl.semaphore_signal(barrier, inc=1, device_id=peer, device_id_type=MESH)
 
+    a1, a2 = s["a1"], s["a2"]
+    down = one_hot(iota((PAD, ROWS), 0) == iota((PAD, ROWS), 1))
+    keys, values = dot_nn(down, wk_ref[...]), dot_nn(down, wv_ref[...])
+    a1[place.dp, :, pl.ds(0, 384)] = jnp.concatenate([keys, values], axis=1).astype(BF16)
+    query = dot_nn(down, wq_ref[...])
+    a1[place.dp, :, pl.ds(384, 512)] = query[:, 0:512].astype(BF16)
+    row = iota((128, ROWS), 0)
+    gains = jnp.where(row == 64, na_ref[...], jnp.where(row == 65, nm_ref[...], 0.0)).astype(BF16)
+    tail = jnp.concatenate([query[:, 512:576], jnp.zeros((PAD, 64), F32)], axis=1)
+    a1[place.dp, :, pl.ds(896, 128)] = (tail + dot_nt(down, gains)).astype(BF16)
+    a2[place.dp] = dot_nn(down, wo_ref[...]).astype(BF16)
+
     row, col = iota((16, 12), 0), iota((16, 12), 1)
-    down = wd_ref[...]
     for p in range(3):
         tile = jnp.zeros((16, D), F32)
         for t, ref in enumerate((wg_ref, wu_ref, wd_ref)):
             pick = one_hot(((row >> 2) == t) & (col == 4 * p + (row & 3)))
-            tile += dot_nn(pick, down) if t == 2 else dot_nt(pick, ref[...])
+            tile += dot_nn(pick, ref[...])
         s["tile"][p] = tile.astype(BF16)
 
     pl.semaphore_wait(barrier, len(peers))
 
-    a1, a2 = s["a1"], s["a2"]
-    other_dp = place.other_core()[0]
-    a_slots = {}
-    for name, ref, whole in (("a1", a1_ref, a1), ("a2", a2_ref, a2)):
-        group_slots = [net.new() for _ in GROUP_STEPS]
-        core_slots = [net.new() for _ in range(8)]
-        a_slots[name] = (group_slots, core_slots)
+    first_weights, out_weights = Gathered(net, place, a1), Gathered(net, place, a2)
     ff_slots = [[[net.new() for _ in range(3)] for _ in range(3)] for _ in range(3)]
     dy_slot, n2_slot, out_slot, dn2_slot = (net.new() for _ in range(4))
-
-    def send_own(name, ref, whole):
-        group_slots, core_slots = a_slots[name]
-        for k, (dz, dx) in enumerate(GROUP_STEPS):
-            net.start(group_slots[k], ref, whole.at[place.dp], place.group(dz, dx)[0])
-        net.start(core_slots[7], ref, whole.at[place.dp], place.other_core())
-        whole[place.dp] = ref[...]
-
-    def pass_on(name, whole):
-        group_slots, core_slots = a_slots[name]
-        for k, (dz, dx) in enumerate(GROUP_STEPS):
-            device, index = place.group(-dz, dx)
-            block = whole.at[index * 2 + place.core]
-            net.arrived(group_slots[k], block, device)
-            net.start(core_slots[k], block, block, place.other_core())
-
-    def have_all(name, whole):
-        group_slots, core_slots = a_slots[name]
-        for k, (dz, dx) in enumerate(GROUP_STEPS):
-            _, index = place.group(-dz, dx)
-            net.arrived(core_slots[k], whole.at[index * 2 + 1 - place.core], place.other_core())
-        net.arrived(core_slots[7], whole.at[other_dp], place.other_core())
-
-    send_own("a1", a1_ref, a1)
+    first_weights.begin()
     for p, (one, _, _) in enumerate(ORDERS):
         mine = place.coordinate(one)
         s["first"][p, mine] = s["tile"][p]
@@ -237,8 +350,9 @@
             net.start(
                 ff_slots[p][0][d - 1], s["tile"].at[p], s["first"].at[p, mine], place.ring(one, d)
             )
-    send_own("a2", a2_ref, a2)
-    s["dy"][0] = dy_ref[...].reshape(256, D)
+    for b in range(2):
+        s["x"][pl.ds(128 * b, 128)] = jnp.transpose(x_ref[b].astype(F32)).astype(BF16)
+        s["dy"][0, pl.ds(128 * b, 128)] = jnp.transpose(dy_ref[b].astype(F32)).astype(BF16)
     net.start(dy_slot, s["dy"].at[0], s["dy"].at[1], place.other_core())
 
     row = iota((D, DP_ROWS), 0).astype(F32)
@@ -263,7 +377,7 @@
             s["bias"][b, :, pl.ds(128 * k, 128)] = jnp.where(
                 (key >= begin) & (key <= here), 0.0, MASKED
             )
-    x = x_ref[...].reshape(256, D)
+    x = s["x"][...]
     x32 = x.astype(F32)
     inv1 = lax.rsqrt(jnp.sum(x32 * x32, axis=1, keepdims=True) * (1.0 / D) + NORM_EPS)
     s["inv1"][...] = inv1
@@ -291,16 +405,16 @@
             for d in (1, 2, 3):
                 net.start(ff_slots[p][1][d - 1], block, block, place.ring(two, d))
 
-    def ff_third():
-        for p, (_, two, three) in enumerate(ORDERS):
-            mine, last = place.coordinate(two), place.coordinate(three)
-            for d in (1, 2, 3):
-                net.arrived(
-                    ff_slots[p][1][d - 1], s["w"].at[p, last, (mine + 4 - d) % 4], place.ring(two, -d)
-                )
-            block = s["w"].at[p, last]
-            for d in (1, 2, 3):
-                net.start(ff_slots[p][2][d - 1], block, block, place.ring(three, d))
+    def ff_third(p):
+        _, two, three = ORDERS[p]
+        mine, last = place.coordinate(two), place.coordinate(three)
+        for d in (1, 2, 3):
+            net.arrived(
+                ff_slots[p][1][d - 1], s["w"].at[p, last, (mine + 4 - d) % 4], place.ring(two, -d)
+            )
+        block = s["w"].at[p, last]
+        for d in (1, 2, 3):
+            net.start(ff_slots[p][2][d - 1], block, block, place.ring(three, d))
 
     def ff_have(p):
         three = ORDERS[p][2]
@@ -311,8 +425,8 @@
             )
 
     ff_second()
-    pass_on("a1", a1)
-    have_all("a1", a1)
+    first_weights.pass_on()
+    first_weights.finish()
 
     gains = jnp.transpose(a1[:, :, pl.ds(896, 128)].reshape(DP_ROWS, 128).astype(F32))
     gain1 = gains[64:65]
@@ -334,18 +448,31 @@
             tile = (tile * HEAD_WIDTH**-0.5).astype(BF16).reshape(2, 128, 128)
             s["q"][:, :, pl.ds(128 * t - 384, 128)] = tile
 
-    kv_slots = [net.new() for _ in range(7)]
-    kv_copies = []
+    kv, apart = s["kv"], place.x_lo == 0
+    kv_slots = [net.new() for _ in range(8)]
+    column_slots = [net.new() for _ in range(8)]
+    across_slots = [net.new() for _ in range(8)]
+    for k in (2, 4, 6):
+        net.start_if(rank + k <= 7, column_slots[k], kv.at[0, 1], kv.at[k, 1], place.rank(k))
+    net.start_if(apart, across_slots[1], kv.at[0, 1], kv.at[1, 1], place.pair())
     for k in range(1, 8):
-        copy = net.copy(kv_slots[k - 1], s["kv"].at[0], s["kv"].at[k], place.rank(k))
-        kv_copies.append(copy)
-        pl.when(rank + k <= 7)(copy.start)
-    ff_third()
-    pass_on("a2", a2)
+        net.start_if(rank + k <= 7, kv_slots[k], kv.at[0, 0], kv.at[k, 0], place.rank(k))
+    out_weights.begin()
+    for k in (2, 6, 4):
+        net.arrived_if(k <= rank, column_slots[k], kv.at[k, 1], place.rank(-k))
+        here = k <= rank
+        net.start_if(here & apart, across_slots[k + 1], kv.at[k, 1], kv.at[k + 1, 1], place.pair())
+        net.start_if(
+            here & jnp.logical_not(apart), across_slots[k - 1], kv.at[k, 1], kv.at[k - 1, 1], place.pair()
+        )
+    ff_third(0)
+    out_weights.pass_on()
     for k in range(1, 8):
-        pl.when(k <= rank)(
-            functools.partial(net.arrived, kv_slots[k - 1], s["kv"].at[k], place.rank(-k))
-        )
+        net.arrived_if(k <= rank, kv_slots[k], kv.at[k, 0], place.rank(-k))
+    for k in (1, 3, 5, 7):
+        net.arrived_if(k <= rank, across_slots[k], kv.at[k, 1], place.pair())
+    ff_third(1)
+    ff_third(2)
 
     def heads(value, group):
         return jnp.concatenate(
@@ -370,10 +497,10 @@
             for h in range(3):
                 s["mixed"][b, :, pl.ds(64 * (3 * g + h), 64)] = mixed[128 * h : 128 * h + 128]
 
-    have_all("a2", a2)
+    out_weights.finish()
     w_out = a2[...].reshape(DP_ROWS, D)
     s["mixed_spread"][...] = dot_nn(s["mixed"][...].reshape(256, D), s["spread"][...]).astype(BF16)
-    middle = x_ref[...].reshape(256, D).astype(F32) + dot_nn(s["mixed_spread"][...], w_out)
+    middle = s["x"][...].astype(F32) + dot_nn(s["mixed_spread"][...], w_out)
     s["middle"][...] = middle
     inv2 = lax.rsqrt(jnp.sum(middle * middle, axis=1, keepdims=True) * (1.0 / D) + NORM_EPS)
     s["inv2"][...] = inv2
@@ -384,7 +511,7 @@
 
     rs_slots = [[[net.new() for _ in range(3)] for _ in range(3)] for _ in range(3)]
     normed, upper = s["n2"][...].reshape(512, D), s["dy"][...].reshape(512, D)
-    for p in range(3):
+    for p in (0, 2, 1):
         ff_have(p)
         w_gate, w_up, w_down = (
             s["w"][p, :, :, pl.ds(16 * t, 16), :].reshape(256, D) for t in range(3)
@@ -409,14 +536,15 @@
             s["g"][p, :, :, pl.ds(16 * t, 16), :] = (
                 dot_tn(left, right).astype(BF16).reshape(4, 4, 16, D)
             )
-        three = ORDERS[p][2]
-        last = place.coordinate(three)
+        first = BACK[p][0]
+        mine = place.coordinate(first)
         for d in (1, 2, 3):
+            there = (mine + d) % 4
             net.start(
                 rs_slots[p][0][d - 1],
-                s["g"].at[p, (last + d) % 4],
+                s["g"].at[p, there] if first == ORDERS[p][2] else s["g"].at[p, :, there],
                 s["ra"].at[p, d - 1],
-                place.ring(three, d),
+                place.ring(first, d),
             )
     s["dn2_out"][...] = s["dn2"][pl.ds(256, 256)].astype(BF16)
     net.start(dn2_slot, s["dn2_out"], s["dn2_in"], place.other_core())
@@ -424,27 +552,29 @@
     net.start(out_slot, s["ahead_out"], s["ahead_in"], place.other_core())
 
     def rs_second():
-        for p, (_, two, three) in enumerate(ORDERS):
+        for p, (first, second) in enumerate(BACK):
             for d in (1, 2, 3):
-                net.arrived(rs_slots[p][0][d - 1], s["ra"].at[p, d - 1], place.ring(three, -d))
-            total = s["g"][p, place.coordinate(three)].astype(F32)
+                net.arrived(rs_slots[p][0][d - 1], s["ra"].at[p, d - 1], place.ring(first, -d))
+            here = place.coordinate(first)
+            total = (s["g"][p, here] if first == ORDERS[p][2] else s["g"][p, :, here]).astype(F32)
             for d in range(3):
                 total += s["ra"][p, d].astype(F32)
             s["s2"][p] = total.astype(BF16)
-            mine = place.coordinate(two)
+            mine = place.coordinate(second)
             for d in (1, 2, 3):
                 net.start(
                     rs_slots[p][1][d - 1],
                     s["s2"].at[p, (mine + d) % 4],
                     s["rb"].at[p, d - 1],
-                    place.ring(two, d),
+                    place.ring(second, d),
                 )
 
     def rs_third():
-        for p, (one, two, _) in enumerate(ORDERS):
+        for p, (_, second) in enumerate(BACK):
+            one = ORDERS[p][0]
             for d in (1, 2, 3):
-                net.arrived(rs_slots[p][1][d - 1], s["rb"].at[p, d - 1], place.ring(two, -d))
-            total = s["s2"][p, place.coordinate(two)].astype(F32)
+                net.arrived(rs_slots[p][1][d - 1], s["rb"].at[p, d - 1], place.ring(second, -d))
+            total = s["s2"][p, place.coordinate(second)].astype(F32)
             for d in range(3):
                 total += s["rb"][p, d].astype(F32)
             s["u"][p] = dot_nn(unpack, total.astype(BF16)).astype(BF16).reshape(4, 16, D)
@@ -479,14 +609,18 @@
     w_out = a2[...].reshape(DP_ROWS, D)
     d_mixed = dot_nt(d_branch, w_out).astype(BF16)
     s["d_mixed"][...] = dot_nt(d_mixed, s["spread"][...]).astype(BF16).reshape(2, 128, D)
-    out_sum = Summed(net, place, s["sum_out"])
-    grad = dot_tn(s["mixed_spread"][...], d_branch).astype(BF16).reshape(8, 2, PAD, D)
-    for c in range(2):
-        s["sum_out"][0][c] = grad[:, c]
+    out_sum = SplitSummed(net, place, s["sum_out"])
+    rest_sum = Summed(net, place, s["sum_rest"])
+    grad = dot_tn(s["mixed_spread"][...], d_branch)
+    out_sum.fill(grad[:, 0:512])
+    rest_sum.fill(0, grad[:, 512:576])
     out_sum.begin()
 
-    dkv_slots = [[net.new() for _ in range(7)] for _ in range(2)]
-    dkv_copies = []
+    dkv, dkv_in = s["dkv"], s["dkv_in"]
+    dkv_slots = [net.new() for _ in range(8)]
+    own_slots = [net.new() for _ in range(8)]
+    relay_slots = [net.new() for _ in range(8)]
+    across_slot = net.new()
     for b in range(2):
         for g in range(3):
             inv = s["inv_sum"][b, g]
@@ -506,18 +640,33 @@
             d_values = jnp.transpose(dot_tn(d_out, weight)).astype(BF16)
             s["dkv"][:, b, :, pl.ds(64 * g, 64)] = d_keys.reshape(8, 128, 64)
             s["dkv"][:, b, :, pl.ds(192 + 64 * g, 64)] = d_values.reshape(8, 128, 64)
-        for k in range(1, 8):
-            copy = net.copy(
-                dkv_slots[b][k - 1], s["dkv"].at[k, b], s["dkv_in"].at[k, b], place.rank(-k)
-            )
-            dkv_copies.append((k, copy))
-            pl.when(k <= rank)(copy.start)
         if b == 0:
-            out_sum.over_group()
+            for k in (2, 4, 6):
+                net.start_if(k <= rank, own_slots[k], dkv.at[k, 0], dkv_in.at[k, 0], place.rank(-k))
+                other = k - 1 + 2 * place.x_lo
+                net.start_if(
+                    k <= rank, relay_slots[k], dkv.at[other, 0], s["relay"].at[k // 2 - 1], place.rank(-k)
+                )
+        else:
+            for k in range(1, 8):
+                net.start_if(k <= rank, dkv_slots[k], dkv.at[k, 1], dkv_in.at[k, 1], place.rank(-k))
+        if b == 0:
+            out_sum.over_y()
             rs_second()
+    s["relay_sum"][...] = jnp.where(place.x_lo == 1, dkv[1, 0].astype(F32), 0.0)
+    for k in (2, 4, 6):
+
+        @pl.when(rank + k <= 7)
+        def _(k=k):
+            net.arrived(relay_slots[k], s["relay"].at[k // 2 - 1], place.rank(k))
+            s["relay_sum"][...] += s["relay"][k // 2 - 1].astype(F32)
+
+    s["across"][...] = s["relay_sum"][...].astype(BF16)
+    net.start(across_slot, s["across"], s["across_in"], place.pair())
     net.arrived(out_slot, s["ahead_in"], place.other_core())
     out = s["middle"][...] + s["ahead"][pl.ds(0, 256)] + s["ahead_in"][...].astype(F32)
-    out_ref[...] = out.astype(BF16).reshape(2, 128, D)
+    for b in range(2):
+        out_ref[b] = jnp.transpose(out[128 * b : 128 * b + 128]).astype(BF16)
 
     cos, sin = s["cos"][...], s["sin"][...]
     lane = iota((256, 128), 1)
@@ -530,25 +679,30 @@
         tile = tile * cos - swap_halves(tile) * sin
         s["dqkv"][:, pl.ds(384 + 128 * t, 128)] = tile.astype(BF16)
     n1 = s["n1"][...]
-    q_sum = Summed(net, place, s["sum_q"])
-    grad = dot_tn(n1, s["dqkv"][:, pl.ds(384, 512)]).astype(BF16).reshape(8, 2, PAD, 512)
-    for c in range(2):
-        s["sum_q"][0][c] = grad[:, c]
+    q_sum = SplitSummed(net, place, s["sum_q"])
+    q_sum.fill(dot_tn(n1, s["dqkv"][:, pl.ds(384, 512)]))
+    rest_sum.fill(64, dot_tn(n1, s["dqkv"][:, pl.ds(896, 128)])[:, 0:64])
     q_sum.begin()
-    out_sum.over_ranks()
+    rest_sum.begin()
+    out_sum.over_group()
     rs_third()
-    q_sum.over_group()
+    q_sum.over_y()
+    rest_sum.over_group()
 
     for b in range(2):
-        s["dkv_sum"][b] = s["dkv"][0, b].astype(F32)
+        s["dkv_sum"][b] = dkv[0, b].astype(F32)
     for k in range(1, 8):
 
         @pl.when(rank + k <= 7)
         def _(k=k):
-            for b in range(2):
-                net.arrived(dkv_slots[b][k - 1], s["dkv_in"].at[k, b], place.rank(k))
-            s["dkv_sum"][...] += s["dkv_in"][k].astype(F32)
-
+            net.arrived(dkv_slots[k], dkv_in.at[k, 1], place.rank(k))
+            s["dkv_sum"][1] += dkv_in[k, 1].astype(F32)
+            if k % 2 == 0:
+                net.arrived(own_slots[k], dkv_in.at[k, 0], place.rank(k))
+                s["dkv_sum"][0] += dkv_in[k, 0].astype(F32)
+
+    net.arrived(across_slot, s["across_in"], place.pair())
+    s["dkv_sum"][0] += s["across_in"][...].astype(F32)
     for t in range(3):
         tile = s["dkv_sum"][:, :, pl.ds(128 * t, 128)].reshape(256, 128)
         if t < 2:
@@ -562,14 +716,19 @@
     spread = s["spread"][...]
     g_gain2 = dot_nn(jnp.broadcast_to(g_gain2, (16, D)).astype(BF16), spread)[0:1]
     row = iota((128, DP_ROWS), 0)
-    g_gains = jnp.transpose(jnp.where(row == 64, g_gain1, jnp.where(row == 65, g_gain2, 0.0)))
+    g_gains = jnp.transpose(jnp.where(row == 0, g_gain1, jnp.where(row == 1, g_gain2, 0.0)))
+    row, col = iota((DP_ROWS, 128), 0).astype(F32), iota((DP_ROWS, 128), 1).astype(F32)
+    within = row - PAD * jnp.floor((row + 0.5) * (1.0 / PAD)) == col
+    row, col = iota((BLOCKS, DP_ROWS), 0), iota((BLOCKS, DP_ROWS), 1)
+    block = one_hot((col >= row * PAD) & (col < row * PAD + PAD))
+    lines = [dot_nn(block, jnp.where(within, g_gains[:, k : k + 1], 0.0).astype(BF16)) for k in range(2)]
+    row, col = iota((DP_ROWS, 2 * BLOCKS), 0), iota((DP_ROWS, 2 * BLOCKS), 1)
+    put = one_hot(row == (col & 15) * PAD + ROWS + (col >> 4))
+    lines = dot_nn(put, jnp.concatenate(lines, axis=0).astype(BF16))
     t_sum = Summed(net, place, s["sum_t"])
-    grad = dot_tn(n1, d_pre[:, 0:384]).astype(BF16).reshape(8, 2, PAD, 384)
-    rest = dot_tn(n1, d_pre[:, 896:1024]) + g_gains
-    rest = rest.astype(BF16).reshape(8, 2, PAD, 128)
-    for c in range(2):
-        s["sum_t"][0][c, :, :, pl.ds(0, 384)] = grad[:, c]
-        s["sum_t"][0][c, :, :, pl.ds(384, 128)] = rest[:, c]
+    grad = dot_tn(n1, d_pre[:, 0:384])
+    t_sum.fill(0, grad[:, 0:128] + lines)
+    t_sum.fill(128, grad[:, 128:384])
     t_sum.begin()
 
     scaled = d_normed * s["gain1"][...]
@@ -578,38 +737,37 @@
     high = d_in.astype(BF16)
     low = (d_in - high.astype(F32)).astype(BF16)
     d_in = s["d_middle"][...] + dot_nt(high, spread) + dot_nt(low, spread)
-    gx_ref[...] = d_in.astype(BF16).reshape(2, 128, D)
-
     t_sum.over_group()
-    q_sum.over_ranks()
+    for b in range(2):
+        gx_ref[b] = jnp.transpose(d_in[128 * b : 128 * b + 128]).astype(BF16)
+    out_sum.over_pair()
+    q_sum.over_group()
+    rest_sum.over_ranks()
     rs_result()
     sums = s["f"][...]
     high = sums.astype(BF16)
     low = (sums - high.astype(F32)).astype(BF16)
-    row, col = iota((PAD, 12), 0), iota((PAD, 12), 1)
-    for t, ref in enumerate((gg_ref, gu_ref)):
-        pick = one_hot(row == ((col >> 2) << 4) + 4 * t + (col & 3))
-        ref[...] = dot_tn(high, pick) + dot_tn(low, pick)
     row, col = iota((12, PAD), 0), iota((12, PAD), 1)
-    pick = one_hot(col == ((row >> 2) << 4) + 8 + (row & 3))
-    gd_ref[...] = dot_nn(pick, high) + dot_nn(pick, low)
-    go_ref[...] = out_sum.result()[0:ROWS]
+    for t, ref in enumerate((gg_ref, gu_ref, gd_ref)):
+        pick = one_hot(col == ((row >> 2) << 4) + 4 * t + (row & 3))
+        ref[...] = dot_nn(pick, high) + dot_nn(pick, low)
+    out_sum.back()
+    q_sum.over_pair()
     t_sum.over_ranks()
-    total = q_sum.result()
-    gq_ref[:, pl.ds(0, 512)] = total[0:ROWS]
+    q_sum.back()
+    total = rest_sum.result()
+    go_ref[:, pl.ds(512, 64)] = total[0:ROWS, 0:64]
+    gq_ref[:, pl.ds(512, 64)] = total[0:ROWS, 64:128]
+    out_sum.result(go_ref)
+    q_sum.result(gq_ref)
     total = t_sum.result()
     gk_ref[...] = total[0:ROWS, 0:192]
     gv_ref[...] = total[0:ROWS, 192:384]
-    gq_ref[:, pl.ds(512, 64)] = total[0:ROWS, 384:448]
-    across = jnp.transpose(total[:, 384:512])
-    gna_ref[...] = across[64:65, 0:ROWS]
-    gnm_ref[...] = across[65:66, 0:ROWS]
-
+    gna_ref[...] = total[ROWS : ROWS + 1, 0:ROWS]
+    gnm_ref[...] = total[ROWS + 1 : ROWS + 2, 0:ROWS]
+
+    assert net.used <= COPIES, net.used
     net.finish()
-    for k, copy in enumerate(kv_copies, 1):
-        pl.when(rank + k <= 7)(copy.wait_send)
-    for k, copy in dkv_copies:
-        pl.when(k <= rank)(copy.wait_send)
 
 
 def sum_buffers(width):
@@ -623,11 +781,27 @@
     ]
 
 
-COPIES = 160
+def split_buffers():
+    shapes = [
+        (2, 4, 8, PAD, 128),
+        (4, 8, PAD, 128),
+        (4, 8, PAD, 128),
+        (3, 8, PAD, 128),
+        (8, PAD, 128),
+        (7, PAD, 128),
+        (PAD, 128),
+        (PAD, 128),
+        (4, PAD, 128),
+    ]
+    return [pltpu.VMEM(shape, BF16) for shape in shapes]
+
+
+COPIES = 200
 
 SCRATCH = {
     "send": pltpu.SemaphoreType.DMA((COPIES,)),
     "recv": pltpu.SemaphoreType.DMA((COPIES,)),
+    "x": pltpu.VMEM((256, D), BF16),
     "tile": pltpu.VMEM((3, 16, D), BF16),
     "first": pltpu.VMEM((3, 4, 16, D), BF16),
     "w": pltpu.VMEM((3, 4, 4, PAD, D), BF16),
@@ -663,6 +837,10 @@
     "dq": pltpu.VMEM((2, 128, D), F32),
     "dkv": pltpu.VMEM((8, 2, 128, 384), BF16),
     "dkv_in": pltpu.VMEM((8, 2, 128, 384), BF16),
+    "relay": pltpu.VMEM((3, 128, 384), BF16),
+    "relay_sum": pltpu.VMEM((128, 384), F32),
+    "across": pltpu.VMEM((128, 384), BF16),
+    "across_in": pltpu.VMEM((128, 384), BF16),
     "dkv_sum": pltpu.VMEM((2, 128, 384), F32),
     "dqkv": pltpu.VMEM((256, 1024), BF16),
     "g": pltpu.VMEM((3, 4, 4, PAD, D), BF16),
@@ -672,47 +850,68 @@
     "u": pltpu.VMEM((3, 4, 16, D), BF16),
     "rc": pltpu.VMEM((3, 3, 16, D), BF16),
     "f": pltpu.VMEM((PAD, D), F32),
-    "sum_out": sum_buffers(D),
-    "sum_q": sum_buffers(512),
-    "sum_t": sum_buffers(512),
+    "sum_out": split_buffers(),
+    "sum_q": split_buffers(),
+    "sum_rest": sum_buffers(128),
+    "sum_t": sum_buffers(384),
 }
+
+
+def hand_over(*refs):
+    count = len(refs) // 2
+    for a, b in zip(refs[:count], refs[count:]):
+        b[...] = a[...]
 
 
 def local(
     inputs, segment_ids, norm_attn, w_query, w_key, w_value, w_out, norm_mlp, w_gate, w_up, w_down, cotangent,
 ):
-    columns = [w_key, w_value, w_query, norm_attn[:, None], norm_mlp[:, None]]
-    a1 = jnp.pad(jnp.concatenate(columns, axis=1), ((0, PAD - ROWS), (0, 62)))
-    a2 = jnp.pad(w_out, ((0, PAD - ROWS), (0, 0)))
     half = HEAD_WIDTH // 2
-    freq = ROPE_BASE ** (-(2.0 * jnp.arange(half, dtype=F32)) / HEAD_WIDTH)
-    freq = jnp.tile(freq, 4)[None, :]
+    freq = np.float32(ROPE_BASE) ** (-(np.float32(2.0) * np.arange(half, dtype=np.float32)) / HEAD_WIDTH)
+    freq = jnp.asarray(np.tile(freq.astype(np.float32), 4)[None, :])
     shapes = [
-        ((2, 128, D), BF16),
-        ((2, 128, D), BF16),
+        ((2, D, 128), BF16),
+        ((2, D, 128), BF16),
         ((1, ROWS), F32),
         ((ROWS, 576), F32),
         ((ROWS, 192), F32),
         ((ROWS, 192), F32),
         ((ROWS, D), F32),
         ((1, ROWS), F32),
-        ((D, 12), F32),
-        ((D, 12), F32),
+        ((12, D), F32),
+        ((12, D), F32),
         ((12, D), F32),
     ]
+    shapes = [jax.ShapeDtypeStruct(shape, dtype) for shape, dtype in shapes]
+    count = len(shapes)
     outs = pl.pallas_call(
         kernel,
-        out_shape=[jax.ShapeDtypeStruct(shape, dtype) for shape, dtype in shapes],
-        in_specs=[pl.BlockSpec(memory_space=pltpu.VMEM)] * 9,
-        out_specs=[pl.BlockSpec(memory_space=pltpu.VMEM)] * len(shapes),
+        out_shape=shapes,
+        in_specs=[pl.BlockSpec(memory_space=pltpu.VMEM)] * 13,
+        out_specs=[pl.BlockSpec(memory_space=pltpu.VMEM)] * count,
         scratch_shapes=[SCRATCH],
         compiler_params=pltpu.CompilerParams(
             collective_id=0, has_side_effects=True, vmem_limit_bytes=60 * 2**20
         ),
         name="layer",
-    )(inputs, segment_ids, a1, a2, w_gate, w_up, w_down, cotangent, freq)
+    )(
+        jnp.transpose(inputs, (0, 2, 1)), segment_ids, norm_attn[None, :], w_query, w_key, w_value, w_out,
+        norm_mlp[None, :], w_gate.T, w_up.T, w_down, jnp.transpose(cotangent, (0, 2, 1)), freq,
+    )
+    outs = pl.pallas_call(
+        hand_over,
+        out_shape=shapes,
+        in_specs=[pl.BlockSpec(memory_space=pltpu.VMEM)] * count,
+        out_specs=[pl.BlockSpec(memory_space=pltpu.VMEM)] * count,
+        name="hand_over",
+    )(*outs)
     outs = list(outs)
-    outs[2], outs[7] = outs[2].reshape(ROWS), outs[7].reshape(ROWS)
+    for k in (0, 1):
+        outs[k] = jnp.transpose(outs[k], (0, 2, 1))
+    for k in (2, 7):
+        outs[k] = outs[k].reshape(ROWS)
+    for k in (8, 9):
+        outs[k] = outs[k].T
     return tuple(outs)
 
 

time: 142 us -> 121 us (0.85); the launches traced: 140 us -> 121 us
  local copies, waits for them, and re-layouts: 15.9 us -> 0 us
  Pallas kernels: 123 us -> 120 us
    unnamed x49 -> x0, local copies, waits for them, and re-layouts: 12.2 us -> none
    pallas_call x1 -> x2, Pallas kernels: 123 us -> 120 us  [the longest x1 118 us: local(): pl.pallas_call(kernel, out_shape=shapes, in_specs=[pl.BlockSpec(memory_sp...]
where the time goes in v2:
time: 121 us
  Pallas kernels  120 us (99%)
    pallas_call x1, Pallas kernels, local(): pl.pallas_call(kernel, out_shape=shapes, in_specs=[pl.BlockSpec(memory_sp...  118 us

profile of v2, /device:TPU:2, one launch (start us, length us, event | category | flops | bytes accessed | tf_op | source)
XLA Modules:
  0.0 120.9 jit_solution(17025374505816945470)
XLA Ops:
  0.6 117.9 %layer.1 = (bf16[2,576,128]{2,1,0:T(8,128)(2,1)}, bf16[2,576,128]{2,1,0:T(8,128)(2,1)}, f32[1,36]{1,0:T(1,128)}, f32[36,576]{1,0:T(8,128)}, f32[36,192]{1,0:T(8,...) custom-call(bf16[2,576,128]{2,1,0:T(8,128)(2,1)} %bitcast.12, ...), custom_call_target="tpu_custom_call" | custom-call | tf_op jit(solution)/shard_map/layer/pallas_call | solution.py:887
  118.6 2.2 %hand_over.1 = (bf16[2,576,128]{2,1,0:T(8,128)(2,1)}, bf16[2,576,128]{2,1,0:T(8,128)(2,1)}, f32[1,36]{1,0:T(1,128)}, f32[36,576]{1,0:T(8,128)}, f32[36,192]{1,0:...) custom-call(bf16[2,576,128]{2,1,0:T(8,128)(2,1)} %get-tuple-element., ...), custom_call_target="tpu_custom_call" | custom-call | tf_op jit(solution)/shard_map/hand_over/pallas_call | solution.py:901
